TPU v7x, 256 devices: a whole 4x4x8 slice. The times are simulated.
256 devices in a mesh: subj: 32 (over y, z), var: 8 (over x, core).
Axes of the slice: x: 4, y: 4, z: 8, core: 2. Of those that a mesh axis runs over, the one named last changes fastest.
Arguments:
- genotype: bfloat16 [32768, 32768], P('subj', 'var'), may hold values from -6 to 6
- coefs: bfloat16 [32768, 48], P('var'), may hold values from -0.03125 to 0.03125
- events: int32 [32768], P('subj'), may hold values 0 or 1
- folds: int32 [32768, 48], P('subj'), may hold values 0 or 1
- groups: int32 [32768], P('subj'), may hold values from 0 to 2015, as said below
Outputs:
- gradient: float32 [32768, 48], P(('var', 'subj'))
Inputs may be any that keep to these rules, and one draw needn't show every extreme that they name: groups never fall along the subjects; every group holds 1 to 32 consecutive subjects; each aligned block of 1024 subjects holds whole groups only, 63 of them, one exactly 32; every group number occurs.
All inputs are finite; a program needn't handle non-finite values. No bound on the sum of `events` or of `folds` on one device may be relied on, other than what follows from the above.
Results may differ from a plain program's by a relative error of at most 0.0026.
Values may be sent and summed in bfloat16 or wider, within the bound.
No kernel may reach another device: no remote copies, remote signals or barrier semaphores. Data moves between devices by JAX's collectives and lax.ppermute only.
A program may use at most 64 MiB of HBM per device.

v0:
```python
import jax
import jax.numpy as jnp
from jax import lax
from jax.sharding import PartitionSpec as P


def carried_in(value, axis, join, neutral, backward):
    count, mine = (lax.axis_size(axis), lax.axis_index(axis))
    pieces = lax.all_gather(value, axis)
    if backward:
        pieces = pieces[::-1]
        mine = count - 1 - mine
    total = jnp.full_like(value, 0) + jnp.asarray(neutral, value.dtype)

    def step(position, total):
        longer = join(total, pieces[position])
        return jnp.where(position < mine, longer, total)

    return lax.fori_loop(0, count - 1, step, total)


def add_pair(earlier, later):
    return earlier + later


def later_total(block_total):
    return carried_in(block_total, "subj", add_pair, jnp.zeros_like(block_total), True)


def earlier_total(block_total):
    return carried_in(block_total, "subj", add_pair, jnp.zeros_like(block_total), False)


def resid_of(eta, fold_cols, events, groups):
    count_rows = groups.shape[0]
    fold_float = fold_cols.astype(jnp.float32)
    risk_weight = fold_float * jnp.exp(eta)
    counted = events.astype(jnp.float32)[:, None] * fold_float
    position = jnp.arange(count_rows, dtype=jnp.int32)
    before_ids = jnp.concatenate([groups[:1] - 1, groups[:-1]])
    after_ids = jnp.concatenate([groups[1:], groups[-1:] + 1])
    start_mark = jnp.where(groups != before_ids, position, 0)
    start_pos = lax.cummax(start_mark, axis=0)
    end_mark = jnp.where(groups != after_ids, position, count_rows - 1)
    finish_pos = lax.cummin(end_mark, axis=0, reverse=True)
    suffix = jnp.cumsum(risk_weight[::-1], axis=0)[::-1]
    local_risk = jnp.take(suffix, start_pos, axis=0)
    carried = later_total(suffix[0])
    risk_sum = carried[None, :] + local_risk
    inverse = counted / jnp.where(counted > 0, risk_sum, 1.0)
    prefix = jnp.cumsum(inverse, axis=0)
    local_hazard = jnp.take(prefix, finish_pos, axis=0)
    before = earlier_total(prefix[-1])
    hazard = before[None, :] + local_hazard
    return (counted - risk_weight * hazard).astype(jnp.bfloat16)


def per_device(genotype, coefs, events, folds, groups):
    partial_eta = jnp.dot(genotype, coefs, preferred_element_type=jnp.float32)
    eta = lax.psum(partial_eta, "var")
    resid = resid_of(eta, folds, events, groups)
    factor = -1.0 / jnp.sqrt(jnp.float32(genotype.shape[0] * lax.axis_size("subj")))
    product = lax.dot_general(
        genotype, resid, (((0,), (0,)), ((), ())), preferred_element_type=jnp.float32
    )
    return lax.psum_scatter(product * factor, "subj", scatter_dimension=0, tiled=True)


def solution(mesh):
    in_specs = (P("subj", "var"), P("var", None), P("subj"), P("subj", None), P("subj"))
    out_specs = P(("var", "subj"), None)
    return jax.shard_map(
        per_device, mesh=mesh, in_specs=in_specs, out_specs=out_specs, check_vma=False
    )
```

profile of v0, /device:TPU:32, one launch (start us, length us, event | category | flops | bytes accessed | tf_op | source)
XLA Modules:
  0.0 405.7 jit_solution(1272700435680269766)
XLA Ops:
  6.5 0.0 copy-start
  6.5 0.0 all-reduce.2.cloned.1.call-start
  6.6 0.9 copy-done
  7.5 6.7 %fusion.17 = f32[1024,48]{0,1:T(8,128)} fusion(bf16[1024,4096]{1,0:T(8,128)(2,1)} %param.11, bf16[4096,48]{0,1:T(8,128)(2,1)S(1)} %copy-done), kind=kOutput, calls=%fused_computation.41 | convolution fusion | flops 402653184 | bytes 8978432 | tf_op jit(solution)/shard_map/dot_general | solution.py:59
  14.2 0.0 all-reduce.2.cloned.1.call-update
  14.2 0.0 reduce-scatter.2.cloned.1.call-start
  14.3 0.0 copy-done.2
  14.3 0.6 fusion.16
  14.9 0.1 fusion.15
  16.2 0.1 select_bitcast_fusion
  16.3 0.3 reduce-window.34
  16.6 0.1 slice.50
  16.7 0.1 slice_reduce_fusion.1
  16.8 0.1 compare_and_fusion.1
  16.9 0.1 fusion.12
  17.0 2.3 reduce-window.48
  19.3 0.1 slice_reduce_fusion
  19.4 0.1 fusion.13
  19.5 0.1 compare_and_fusion
  19.6 0.0 copy-done.3
  19.6 62.1 %all-reduce.2.cloned.1.call-done = f32[1024,48]{0,1:T(8,128)} async-done(((f32[1024,48]{0,1:T(8,128)}), f32[1024,48]{0,1:T(8,128)}) %all-reduce.2.cloned.1.call-update) | async-done | bytes 196624 | tf_op jit(solution)/shard_map/psum | solution.py:60
  81.8 1.0 exponential_multiply_fusion
  82.7 0.6 rev.9
  83.4 13.5 %reduce-window.30 = f32[48,8,128]{2,1,0:T(8,128)S(1)} reduce-window(f32[48,8,128]{2,1,0:T(8,128)S(1)} %bitcast.55, f32[]{:T(128)} %constant.76.clone.1), window={size=1x1x128 pad=0_0x0_0x127_0}, to_apply=%region_1.2 | reduce-window | flops 6242304 | bytes 393220 | tf_op jit(solution)/shard_map/reduce-window
  96.9 0.1 slice.63
  97.0 0.1 copy.18
  97.2 0.1 copy.19
  97.3 0.1 broadcast_add_fusion.1
  97.4 0.2 copy.26
  97.6 0.2 rev.11
  97.9 2.8 gather_fusion
  100.7 0.2 copy.21
  100.9 38.9 %all-gather = f32[32,1,48]{2,1,0:T(1,128)S(1)} all-gather(f32[1,1,48]{2,1,0:T(1,128)S(1)} %slice_bitcast_fusion.1), channel_id=1, replica_groups=mesh['subj'=32,'var'=8] {'subj'}, dimensions={0}, use_global_device_ids=true | all-gather | bytes 6336 | tf_op jit(solution)/shard_map/all_gather | solution.py:9
  139.8 1.2 while.28
  141.1 0.1 fusion.6
  141.2 13.5 %reduce-window.36 = f32[48,8,128]{2,1,0:T(8,128)S(1)} reduce-window(f32[48,8,128]{2,1,0:T(8,128)S(1)} %bitcast.56, f32[]{:T(128)} %constant.76.clone.1), window={size=1x1x128 pad=0_0x0_0x127_0}, to_apply=%region_7.9 | reduce-window | flops 6242304 | bytes 393220 | tf_op jit(solution)/shard_map/reduce-window.4
  154.7 0.1 slice.67
  154.8 0.1 copy.22
  155.0 0.1 copy.23
  155.1 0.1 broadcast_add_fusion
  155.2 0.2 copy.27
  155.5 2.8 gather_fusion.1
  158.3 0.2 copy.25
  158.5 36.6 %all-gather.1 = f32[32,1,48]{2,1,0:T(1,128)S(1)} all-gather(f32[1,1,48]{2,1,0:T(1,128)S(1)} %slice_bitcast_fusion), channel_id=1, replica_groups=mesh['subj'=32,'var'=8] {'subj'}, dimensions={0}, use_global_device_ids=true | all-gather | bytes 6336 | tf_op jit(solution)/shard_map/all_gather | solution.py:9
  195.1 1.2 while.29
  196.3 5.9 %fusion = f32[4096,48]{0,1:T(8,128)} fusion(bf16[1024,4096]{1,0:T(8,128)(2,1)} %param.11, f32[1024,48]{0,1:T(8,128)S(1)} %exponential_multiply_fusion, f32[1024,48]{0,1:T(8,128)S(1)} %copy.25, s32[1024,48]{0,1:T(8,128)S(1)} %copy-done.1, f32[48]{0:T(128)S(1)} %get-tuple-element.165, f32[1024]{0:T(1024)S(1)} %convert_element_type.9, ...), kind=kOutput, calls=%fused_computation.7 | convolution fusion | flops 403193856 | bytes 9770176 | tf_op jit(solution)/shard_map/dot_general | solution.py:63
  202.2 0.0 reduce-scatter.2.cloned.1.call-update
  202.2 196.6 %reduce-scatter.2.cloned.1.call-done = f32[128,48]{0,1:T(8,128)} async-done(((f32[4096,48]{0,1:T(8,128)}), f32[128,48]{0,1:T(8,128)}) %reduce-scatter.2.cloned.1.call-update) | async-done | bytes 24592 | tf_op jit(solution)/shard_map/reduce_scatter | solution.py:66
  (80 shorter events, 1.3 us)
Async XLA Ops:
  6.5 1.0 copy-start
  6.5 7.8 %copy-start.2 = (s32[1024]{0:T(1024)S(1)}, s32[1024]{0:T(1024)}, u32[]{:S(2)}) copy-start(s32[1024]{0:T(1024)} %param.15) | copy-start | bytes 12292
  6.5 13.1 %copy-start.3 = (s32[1024]{0:T(1024)S(1)}, s32[1024]{0:T(1024)}, u32[]{:S(2)}) copy-start(s32[1024]{0:T(1024)} %param.13) | copy-start | bytes 12292
  6.5 75.2 %copy-start.1 = (s32[1024,48]{0,1:T(8,128)S(1)}, s32[1024,48]{0,1:T(8,128)}, u32[]{:S(2)}) copy-start(s32[1024,48]{0,1:T(8,128)} %param.14) | copy-start | bytes 589828
  6.5 75.2 %all-reduce.2.cloned.1.call-start = ((), (), s32[]{:S(2)}) async-start(), calls=%async_computation.1 | async-start | bytes 393216 | tf_op jit(solution)/shard_map/psum | solution.py:60
  14.2 384.6 %reduce-scatter.2.cloned.1.call-start = ((), (), s32[]{:S(2)}) async-start(), calls=%async_computation.2 | async-start | bytes 811008 | tf_op jit(solution)/shard_map/reduce_scatter | solution.py:66
Sparse Core Ops, SparseCore 0:
  14.4 67.3 all-reduce.1
  202.4 196.4 reduce-scatter.1
where the time goes:
time: 407 us; the launch traced here: 406 us
  waiting for transfers between devices  259 us (64%)
  blocking collectives  75.6 us (19%)
  other arithmetic  32.5 us (8%)
  between operations  14.9 us (4%)
  matrix products  12.6 us (3%)
  local copies, waits for them, and re-layouts  9.9 us (2%)
    reduce_scatter x1, waiting for transfers between devices, per_device(): lax.psum_scatter(product * factor, 'subj', scatter_dimension=0, tiled=True)  197 us
    all_gather x2, blocking collectives, carried_in(): pieces = lax.all_gather(value, axis)  75.6 us
    psum x1, waiting for transfers between devices, per_device(): eta = lax.psum(partial_eta, 'var')  62.1 us
    another operation x11, other arithmetic  30.1 us
  transfers between devices with their start and end apart: 2, of which 2 were waited for; matrix products, arithmetic and copies ran while one was open for 1% of the time, Pallas kernels for 0%

commit v1 on v0

v1 whole, which is shorter than its diff:
```python
import functools

import jax
import jax.numpy as jnp
from jax import lax
from jax.experimental import pallas as pl
from jax.experimental.pallas import tpu as pltpu
from jax.sharding import PartitionSpec as P

COLS = 48
OWN = 6
ROWS = 1024
SLOTS = 64
VMEM = 40 * 1024 * 1024

SEND = jnp.bfloat16


def gray(value):
    return value ^ (value >> 1)


def var_label(index):
    return (index & 1) * 4 + gray(index >> 1)


def subj_label(index):
    y = gray(index >> 3)
    z = gray(index & 7)
    return (
        (y & 1) * 16 + (z & 1) * 8 + ((y >> 1) & 1) * 4 + ((z >> 1) & 1) * 2 + ((z >> 2) & 1)
    )


def exchange(value, axis, count, label, mask):
    labels = [label(index) for index in range(count)]
    where = {l: index for index, l in enumerate(labels)}
    pairs = [(index, where[labels[index] ^ mask]) for index in range(count)]
    return lax.ppermute(value, axis, pairs)


def parts3(value):
    high = value.astype(jnp.bfloat16)
    rest = value - high.astype(jnp.float32)
    mid = rest.astype(jnp.bfloat16)
    low = (rest - mid.astype(jnp.float32)).astype(jnp.bfloat16)
    return high, mid, low


def params():
    return pltpu.CompilerParams(vmem_limit_bytes=VMEM)


def one_hot(groups_ref, base):
    slot = lax.broadcasted_iota(jnp.int32, (SLOTS, ROWS), 0)
    return (slot == groups_ref[...] - base).astype(jnp.bfloat16)


def eta_kernel(where_ref, geno_ref, coefs_ref, out_ref):
    label = where_ref[0]
    step = pl.program_id(0)
    width = geno_ref.shape[0]
    block = jnp.dot(geno_ref[...], coefs_ref[...], preferred_element_type=jnp.float32)
    turned = block.T
    at = pl.ds(pl.multiple_of(step * width, 128), width)
    for chunk in range(8):
        out_ref[chunk ^ label, :, at] = turned[OWN * chunk : OWN * chunk + OWN, :]


def eta_slots(where, genotype, coefs):
    rows, depth = genotype.shape
    block = 256
    return pl.pallas_call(
        eta_kernel,
        grid_spec=pltpu.PrefetchScalarGridSpec(
            num_scalar_prefetch=1,
            grid=(rows // block,),
            in_specs=[
                pl.BlockSpec((block, depth), lambda i, w: (i, 0)),
                pl.BlockSpec((depth, COLS), lambda i, w: (0, 0)),
            ],
            out_specs=pl.BlockSpec((8, OWN, rows), lambda i, w: (0, 0, 0)),
        ),
        out_shape=jax.ShapeDtypeStruct((8, OWN, rows), jnp.float32),
        compiler_params=params(),
        cost_estimate=pl.CostEstimate(
            flops=2 * rows * depth * 128, bytes_accessed=rows * depth * 2, transcendentals=0
        ),
    )(where, genotype, coefs)


def count_kernel(where_ref, folds_ref, events_ref, groups_ref, fold_ref, counted_ref, count_ref):
    label = where_ref[0]
    base = where_ref[2]
    row = lax.broadcasted_iota(jnp.int32, (OWN, COLS), 0)
    col = lax.broadcasted_iota(jnp.int32, (OWN, COLS), 1)
    pick = (col == row + OWN * label).astype(jnp.bfloat16)
    fold = lax.dot_general(
        pick,
        folds_ref[...].astype(jnp.bfloat16),
        (((1,), (1,)), ((), ())),
        preferred_element_type=jnp.float32,
    )
    counted = fold * events_ref[...].astype(jnp.float32)
    hot = one_hot(groups_ref, base)
    fold_ref[...] = fold
    counted_ref[...] = counted
    count_ref[...] = lax.dot_general(
        counted.astype(jnp.bfloat16), hot, (((1,), (1,)), ((), ())), preferred_element_type=jnp.float32
    )


def smem():
    return pl.BlockSpec(memory_space=pltpu.SMEM)


def vmem():
    return pl.BlockSpec(memory_space=pltpu.VMEM)


def counts(where, folds, events, groups):
    return pl.pallas_call(
        count_kernel,
        in_specs=[smem(), vmem(), vmem(), vmem()],
        out_specs=[vmem()] * 3,
        out_shape=[
            jax.ShapeDtypeStruct((OWN, ROWS), jnp.float32),
            jax.ShapeDtypeStruct((OWN, ROWS), jnp.float32),
            jax.ShapeDtypeStruct((OWN, SLOTS), jnp.float32),
        ],
        compiler_params=params(),
        cost_estimate=pl.CostEstimate(flops=10**8, bytes_accessed=10**6, transcendentals=0),
    )(where, folds, events, groups)


def weight_kernel(where_ref, eta_ref, more_ref, fold_ref, count_ref, groups_ref, weight_ref, pack_ref):
    base = where_ref[2]
    eta = eta_ref[0] + more_ref[0]
    weight = fold_ref[...] * jnp.exp(eta)
    weight_ref[...] = weight
    hot = one_hot(groups_ref, base)
    total = jnp.zeros((OWN, SLOTS), jnp.float32)
    for part in parts3(weight):
        total += lax.dot_general(
            part, hot, (((1,), (1,)), ((), ())), preferred_element_type=jnp.float32
        )
    pack_ref[0, :, :SLOTS] = total
    pack_ref[0, :, SLOTS:] = count_ref[...]


def weights(where, eta, more, fold, count, groups):
    return pl.pallas_call(
        weight_kernel,
        in_specs=[smem()] + [vmem()] * 5,
        out_specs=[vmem()] * 2,
        out_shape=[
            jax.ShapeDtypeStruct((OWN, ROWS), jnp.float32),
            jax.ShapeDtypeStruct((1, OWN, 2 * SLOTS), jnp.float32),
        ],
        compiler_params=params(),
        cost_estimate=pl.CostEstimate(flops=10**8, bytes_accessed=10**6, transcendentals=0),
    )(where, eta, more, fold, count, groups)


def resid_kernel(where_ref, near_ref, far_ref, weight_ref, counted_ref, groups_ref, resid_ref):
    label = where_ref[1]
    base = where_ref[2]
    mine = where_ref[3]
    half = near_ref.shape[0]
    lane = lax.broadcasted_iota(jnp.int32, (OWN, 2 * SLOTS), 1)
    first = lane < SLOTS
    zero = jnp.zeros((OWN, 2 * SLOTS), jnp.float32)
    after = zero
    before = zero
    own = zero
    for device in reversed(range(2 * half)):
        slot = label ^ subj_label(device)
        low = slot & (half - 1)
        tile = jnp.where(slot < half, near_ref[low], far_ref[low])
        suffix = jnp.where(first, tile, 0.0)
        shift = 1
        while shift < SLOTS:
            suffix = suffix + pltpu.roll(suffix, 2 * SLOTS - shift, 1)
            shift *= 2
        total = suffix + pltpu.roll(suffix, SLOTS, 1)
        count = pltpu.roll(tile, SLOTS, 1)
        some = first & (count > 0)
        risk = jnp.where(some, suffix + after, 1.0)
        added = jnp.where(some, count / risk, 0.0)
        after = after + total
        before = before + jnp.where(device < mine, added, 0.0)
        own = own + jnp.where(device == mine, added, 0.0)
    shift = 1
    prefix = own
    while shift < SLOTS:
        prefix = prefix + pltpu.roll(prefix, shift, 1)
        before = before + pltpu.roll(before, shift, 1)
        shift *= 2
    before = before + pltpu.roll(before, SLOTS, 1)
    hazard = (prefix + before)[:, :SLOTS]
    hot = one_hot(groups_ref, base)
    spread = jnp.zeros((OWN, ROWS), jnp.float32)
    for part in parts3(hazard):
        spread += jnp.dot(part, hot, preferred_element_type=jnp.float32)
    resid = counted_ref[...] - weight_ref[...] * spread
    resid_ref[0] = resid.astype(jnp.bfloat16)


def residuals(where, near, far, weight, counted, groups):
    return pl.pallas_call(
        resid_kernel,
        in_specs=[smem()] + [vmem()] * 5,
        out_specs=vmem(),
        out_shape=jax.ShapeDtypeStruct((1, OWN, ROWS), jnp.bfloat16),
        compiler_params=params(),
        cost_estimate=pl.CostEstimate(flops=10**8, bytes_accessed=10**6, transcendentals=0),
    )(where, near, far, weight, counted, groups)


def grad_kernel(far, factor, where_ref, geno_ref, near_ref, other_ref, out_ref, turned):
    var = where_ref[0]
    label = where_ref[1]
    step = pl.program_id(0)

    @pl.when(step == 0)
    def _():
        for chunk in range(8):
            slot = chunk ^ var
            low = slot & 3
            piece = jnp.where(
                slot < 4, near_ref[low].astype(jnp.float32), other_ref[low].astype(jnp.float32)
            )
            turned[OWN * chunk : OWN * chunk + OWN, :] = piece

    block = jnp.dot(
        turned[...].astype(jnp.bfloat16), geno_ref[...], preferred_element_type=jnp.float32
    )
    block = (block * factor).astype(out_ref.dtype)
    count = geno_ref.shape[1] // 128
    start = block_index(far, step, label, count) * count
    for piece in range(count):
        slot = (subj_label(start + piece) ^ label) & 15
        out_ref[slot] = block[:, 128 * piece : 128 * piece + 128]


def block_index(far, step, label, count):
    per_y = 8 // count
    bit = (label >> 4) & 1
    wanted = bit ^ 1 if far else bit
    y_pick = step // per_y
    y = jnp.where(wanted == 1, 1 + y_pick, 3 * y_pick)
    return y * per_y + lax.rem(step, per_y)


def grad_slots(far, dtype, factor, where, genotype, near, other):
    rows, depth = genotype.shape
    block = 512
    count = block // 128
    return pl.pallas_call(
        functools.partial(grad_kernel, far, factor),
        grid_spec=pltpu.PrefetchScalarGridSpec(
            num_scalar_prefetch=1,
            grid=(depth // block // 2,),
            in_specs=[
                pl.BlockSpec((rows, block), lambda i, w: (0, block_index(far, i, w[1], count))),
                pl.BlockSpec((4, OWN, rows), lambda i, w: (0, 0, 0)),
                pl.BlockSpec((4, OWN, rows), lambda i, w: (0, 0, 0)),
            ],
            out_specs=pl.BlockSpec((16, COLS, 128), lambda i, w: (0, 0, 0)),
            scratch_shapes=[pltpu.VMEM((COLS, rows), jnp.float32)],
        ),
        out_shape=jax.ShapeDtypeStruct((16, COLS, 128), dtype),
        compiler_params=params(),
        cost_estimate=pl.CostEstimate(
            flops=rows * depth * 128, bytes_accessed=rows * depth, transcendentals=0
        ),
    )(where, genotype, near, other)


def per_device(genotype, coefs, events, folds, groups):
    subj = lax.axis_index("subj")
    var = lax.axis_index("var")
    across = functools.partial(exchange, axis="var", count=8, label=var_label)
    along = functools.partial(exchange, axis="subj", count=32, label=subj_label)
    where = jnp.stack(
        [var_label(var), subj_label(subj), subj * 63, subj]
    ).astype(jnp.int32)
    events = events.reshape(1, ROWS)
    groups = groups.reshape(1, ROWS)
    factor = -1.0 / float(32 * ROWS) ** 0.5

    eta = eta_slots(where, genotype, coefs)
    fold, counted, count = counts(where, folds, events, groups)
    eta = eta[:4] + across(eta[4:], mask=4)
    eta = eta[:2] + across(eta[2:], mask=2)
    more = across(eta[1:], mask=1)
    weight, pack = weights(where, eta, more, fold, count, groups)

    for mask in (1, 2, 4, 8):
        pack = jnp.concatenate([pack, along(pack, mask=mask)], axis=0)
    far = along(pack, mask=16)
    resid = residuals(where, pack, far, weight, counted, groups)

    for mask in (1, 2):
        resid = jnp.concatenate([resid, across(resid, mask=mask)], axis=0)
    other = across(resid, mask=4)

    sent = grad_slots(True, SEND, factor, where, genotype, resid, other)
    kept = grad_slots(False, jnp.float32, factor, where, genotype, resid, other)
    total = kept + along(sent, mask=16).astype(jnp.float32)
    for mask in (8, 4, 2, 1):
        out = total[mask:]
        if mask == 8:
            out = out.astype(SEND)
        total = total[:mask] + along(out, mask=mask).astype(jnp.float32)
    return total[0].T


def solution(mesh):
    in_specs = (P("subj", "var"), P("var", None), P("subj"), P("subj", None), P("subj"))
    out_specs = P(("var", "subj"), None)
    return jax.shard_map(
        per_device, mesh=mesh, in_specs=in_specs, out_specs=out_specs, check_vma=False
    )
```

time: 407 us -> 94 us (0.23)
  the two profiles are of different devices: /device:TPU:32 before, /device:TPU:30 now
where the time goes in v1:
time: 94 us; the launch traced here: 93.8 us
  waiting for transfers between devices  57.1 us (61%)
  starting transfers between devices  15.6 us (17%)
  Pallas kernels  11.5 us (12%)
  local copies, waits for them, and re-layouts  8.55 us (9%)
    ppermute x16, waiting for transfers between devices, exchange(): return lax.ppermute(value, axis, pairs)  57.1 us
    ppermute x16, starting transfers between devices, exchange(): return lax.ppermute(value, axis, pairs)  15.6 us
    unnamed x16, local copies, waits for them, and re-layouts  8.49 us
    pallas_call x2, Pallas kernels, grad_slots(): pl.pallas_call(functools.partial(grad_kernel, far, factor), grid_spec=plt...  4.53 us
    pallas_call x1, Pallas kernels, eta_slots(): pl.pallas_call(eta_kernel, grid_spec=pltpu.PrefetchScalarGridSpec(num_sca...  3.59 us
  transfers between devices with their start and end apart: 16, of which 16 were waited for; matrix products, arithmetic and copies ran while one was open for 0% of the time, Pallas kernels for 3%

profile of v1, /device:TPU:30, one launch (start us, length us, event | category | flops | bytes accessed | tf_op | source)
XLA Modules:
  0.0 93.8 jit_solution(17634611307295959052)
XLA Ops:
  0.0 0.0 copy-start.4
  0.0 1.5 %copy.6.coefs_ref = bf16[4096,48]{1,0:T(8,128)(2,1)S(1)} copy(bf16[4096,48]{0,1:T(8,128)(2,1)} %param.6) | data formatting | bytes 786432 | tf_op args[1]
  1.6 0.1 pad_add_fusion.where_ref
  1.7 3.4 %copy-done = bf16[1024,4096]{1,0:T(8,128)(2,1)S(1)} copy-done((bf16[1024,4096]{1,0:T(8,128)(2,1)S(1)}, bf16[1024,4096]{1,0:T(8,128)(2,1)}, u32[]{:S(2)}) %copy-start) | copy-done | bytes 8388632
  5.0 3.6 %shard_map.55 = f32[8,6,1024]{2,1,0:T(8,128)S(1)} custom-call(s32[4]{0:T(128)S(1)} %pad_add_fusion.where_ref, bf16[1024,4096]{1,0:T(8,128)(2,1)S(1)} %copy-done, bf16[4096,48]{1,0:T(8,128)(2,1)S(1)} %copy.6.coefs_ref), custom_call_target="tpu_custom_call" | custom-call | flops 1073741824 | bytes 8388608 | tf_op jit(solution)/shard_map/pallas_call | solution.py:73
  8.7 0.1 collective-permute-start
  8.8 1.3 %collective-permute-done = f32[4,6,1024]{2,1,0:T(8,128)S(1)} collective-permute-done((f32[4,6,1024]{2,1,0:T(8,128)S(1)}, f32[4,6,1024]{2,1,0:T(8,128)S(1)}, u32[]{:S(2)}, u32[]{:S(2)}) %collective-permute-start) | collective-permute-done | bytes 98336 | tf_op jit(solution)/shard_map/ppermute | solution.py:39
  10.1 0.6 collective-permute-start.1
  10.7 5.0 %collective-permute-done.1 = f32[2,6,1024]{2,1,0:T(8,128)S(1)} collective-permute-done((f32[2,6,1024]{2,1,0:T(8,128)S(1)}, f32[2,6,1024]{2,1,0:T(8,128)S(1)}, u32[]{:S(2)}, u32[]{:S(2)}) %collective-permute-start.1) | collective-permute-done | bytes 49184 | tf_op jit(solution)/shard_map/ppermute | solution.py:39
  15.7 0.1 collective-permute-start.2
  15.8 0.0 copy-done.4
  15.8 0.2 copy.7.folds_ref
  16.0 0.0 copy-done.3
  16.0 0.0 copy-done.2
  16.0 0.9 shard_map.56
  16.9 2.8 %collective-permute-done.2.more_ref = f32[1,6,1024]{2,1,0:T(8,128)S(1)} collective-permute-done((f32[1,6,1024]{2,1,0:T(8,128)S(1)}, f32[1,6,1024]{2,1,0:T(8,128)S(1)}, u32[]{:S(2)}, u32[]{:S(2)}) %collective-permute-start.2) | collective-permute-done | bytes 24608 | tf_op jit(solution)/shard_map/ppermute | solution.py:39
  19.7 0.7 shard_map.57
  20.5 5.9 %collective-permute-start.3 = (f32[1,6,128]{2,1,0:T(8,128)S(1)}, f32[1,6,128]{2,1,0:T(8,128)S(1)}, u32[]{:S(2)}, u32[]{:S(2)}) collective-permute-start(f32[1,6,128]{2,1,0:T(8,128)S(1)} %get-tuple-element.12), channel_id=1, source_target_pairs={{0,56},{8,48},{16,40},{24,32},{32,24},{40,16},{48,8},{56,0},{64,12... | collective-permute-start | bytes 9224 | tf_op jit(solution)/shard_map/ppermute | solution.py:39
  26.3 1.6 %collective-permute-done.3 = f32[1,6,128]{2,1,0:T(8,128)S(1)} collective-permute-done((f32[1,6,128]{2,1,0:T(8,128)S(1)}, f32[1,6,128]{2,1,0:T(8,128)S(1)}, u32[]{:S(2)}, u32[]{:S(2)}) %collective-permute-start.3) | collective-permute-done | bytes 3104 | tf_op jit(solution)/shard_map/ppermute | solution.py:39
  27.9 2.0 %collective-permute-start.4 = (f32[2,6,128]{2,1,0:T(8,128)S(1)}, f32[2,6,128]{2,1,0:T(8,128)S(1)}, u32[]{:S(2)}, u32[]{:S(2)}) collective-permute-start(f32[2,6,128]{2,1,0:T(8,128)S(1)} %pad_maximum_fusion.4), channel_id=1, source_target_pairs={{0,24},{8,16},{16,8},{24,0},{32,56},{40,48},{48,40},{56,32},{64,88... | collective-permute-start | bytes 18440 | tf_op jit(solution)/shard_map/ppermute | solution.py:39
  29.9 3.4 %collective-permute-done.4 = f32[2,6,128]{2,1,0:T(8,128)S(1)} collective-permute-done((f32[2,6,128]{2,1,0:T(8,128)S(1)}, f32[2,6,128]{2,1,0:T(8,128)S(1)}, u32[]{:S(2)}, u32[]{:S(2)}) %collective-permute-start.4) | collective-permute-done | bytes 6176 | tf_op jit(solution)/shard_map/ppermute | solution.py:39
  33.4 0.2 collective-permute-start.5
  33.6 4.7 %collective-permute-done.5 = f32[4,6,128]{2,1,0:T(8,128)S(1)} collective-permute-done((f32[4,6,128]{2,1,0:T(8,128)S(1)}, f32[4,6,128]{2,1,0:T(8,128)S(1)}, u32[]{:S(2)}, u32[]{:S(2)}) %collective-permute-start.5) | collective-permute-done | bytes 12320 | tf_op jit(solution)/shard_map/ppermute | solution.py:39
  38.3 0.1 collective-permute-start.6
  38.5 3.8 %collective-permute-done.6 = f32[8,6,128]{2,1,0:T(8,128)S(1)} collective-permute-done((f32[8,6,128]{2,1,0:T(8,128)S(1)}, f32[8,6,128]{2,1,0:T(8,128)S(1)}, u32[]{:S(2)}, u32[]{:S(2)}) %collective-permute-start.6) | collective-permute-done | bytes 24608 | tf_op jit(solution)/shard_map/ppermute | solution.py:39
  42.3 0.0 collective-permute-start.7
  42.3 4.3 %collective-permute-done.7.far_ref = f32[16,6,128]{2,1,0:T(8,128)S(1)} collective-permute-done((f32[16,6,128]{2,1,0:T(8,128)S(1)}, f32[16,6,128]{2,1,0:T(8,128)S(1)}, u32[]{:S(2)}, u32[]{:S(2)}) %collective-permute-start.7) | collective-permute-done | bytes 49184 | tf_op jit(solution)/shard_map/ppermute | solution.py:39
  46.5 1.8 %shard_map.58 = bf16[1,6,1024]{2,1,0:T(8,128)(2,1)S(1)} custom-call(s32[4]{0:T(128)S(1)} %pad_add_fusion.where_ref, f32[16,6,128]{2,1,0:T(8,128)S(1)} %constant_dynamic-update-slice_fusion.near_ref, f32[16,6,128]{2,1,0:T(8,128)S(1)} %collective-permute-done.7.far_ref, f32[6,1024]{1,0:T(8,128)S(1)} %get-tuple-element.13.weight_ref, ...), custom_call_target="tpu_custom_call" | custom-call | flops 100000000 | bytes 1000000 | tf_op jit(solution)/shard_map/pallas_call | solution.py:210
  48.3 0.0 collective-permute-start.8
  48.3 3.7 %collective-permute-done.8 = bf16[1,6,1024]{2,1,0:T(8,128)(2,1)S(1)} collective-permute-done((bf16[1,6,1024]{2,1,0:T(8,128)(2,1)S(1)}, bf16[1,6,1024]{2,1,0:T(8,128)(2,1)S(1)}, u32[]{:S(2)}, u32[]{:S(2)}) %collective-permute-start.8) | collective-permute-done | bytes 12320 | tf_op jit(solution)/shard_map/ppermute | solution.py:39
  52.1 0.6 collective-permute-start.9
  52.6 4.6 %collective-permute-done.9 = bf16[2,6,1024]{2,1,0:T(8,128)(2,1)S(1)} collective-permute-done((bf16[2,6,1024]{2,1,0:T(8,128)(2,1)S(1)}, bf16[2,6,1024]{2,1,0:T(8,128)(2,1)S(1)}, u32[]{:S(2)}, u32[]{:S(2)}) %collective-permute-start.9) | collective-permute-done | bytes 24608 | tf_op jit(solution)/shard_map/ppermute | solution.py:39
  57.3 0.1 collective-permute-start.10
  57.4 1.2 %collective-permute-done.10.other_ref = bf16[4,6,1024]{2,1,0:T(8,128)(2,1)S(1)} collective-permute-done((bf16[4,6,1024]{2,1,0:T(8,128)(2,1)S(1)}, bf16[4,6,1024]{2,1,0:T(8,128)(2,1)S(1)}, u32[]{:S(2)}, u32[]{:S(2)}) %collective-permute-start.10) | collective-permute-done | bytes 49184 | tf_op jit(solution)/shard_map/ppermute | solution.py:39
  58.7 3.4 %copy-done.1 = bf16[1024,4096]{1,0:T(8,128)(2,1)S(1)} copy-done((bf16[1024,4096]{1,0:T(8,128)(2,1)S(1)}, bf16[1024,4096]{1,0:T(8,128)(2,1)}, u32[]{:S(2)}) %copy-start.1) | copy-done | bytes 8388632
  62.0 2.3 %shard_map.60 = bf16[16,48,128]{2,1,0:T(8,128)(2,1)S(1)} custom-call(s32[4]{0:T(128)S(1)} %pad_add_fusion.where_ref, bf16[1024,4096]{1,0:T(8,128)(2,1)S(1)} %copy-done.1, bf16[4,6,1024]{2,1,0:T(8,128)(2,1)S(1)} %pad_maximum_fusion.near_ref, bf16[4,6,1024]{2,1,0:T(8,128)(2,1)S(1)} %collective-permute-done.10.other_ref), custom_call_target="tpu_custom_call" | custom-call | flops 536870912 | bytes 4194304 | tf_op jit(solution)/shard_map/pallas_call | solution.py:259
  64.3 0.1 collective-permute-start.11
  64.4 2.3 %shard_map.59 = f32[16,48,128]{2,1,0:T(8,128)S(1)} custom-call(s32[4]{0:T(128)S(1)} %pad_add_fusion.where_ref, bf16[1024,4096]{1,0:T(8,128)(2,1)S(1)} %copy-done.1, bf16[4,6,1024]{2,1,0:T(8,128)(2,1)S(1)} %pad_maximum_fusion.near_ref, bf16[4,6,1024]{2,1,0:T(8,128)(2,1)S(1)} %collective-permute-done.10.other_ref), custom_call_target="tpu_custom_call" | custom-call | flops 536870912 | bytes 4194304 | tf_op jit(solution)/shard_map/pallas_call | solution.py:259
  66.7 4.7 %collective-permute-done.11 = bf16[16,48,128]{2,1,0:T(8,128)(2,1)S(1)} collective-permute-done((bf16[16,48,128]{2,1,0:T(8,128)(2,1)S(1)}, bf16[16,48,128]{2,1,0:T(8,128)(2,1)S(1)}, u32[]{:S(2)}, u32[]{:S(2)}) %collective-permute-start.11) | collective-permute-done | bytes 196640 | tf_op jit(solution)/shard_map/ppermute | solution.py:39
  71.4 0.2 collective-permute-start.12
  71.6 4.5 %collective-permute-done.12 = bf16[8,48,128]{2,1,0:T(8,128)(2,1)S(1)} collective-permute-done((bf16[8,48,128]{2,1,0:T(8,128)(2,1)S(1)}, bf16[8,48,128]{2,1,0:T(8,128)(2,1)S(1)}, u32[]{:S(2)}, u32[]{:S(2)}) %collective-permute-start.12) | collective-permute-done | bytes 98336 | tf_op jit(solution)/shard_map/ppermute | solution.py:39
  76.2 0.3 collective-permute-start.13
  76.5 5.6 %collective-permute-done.13 = f32[4,48,128]{2,1,0:T(8,128)S(1)} collective-permute-done((f32[4,48,128]{2,1,0:T(8,128)S(1)}, f32[4,48,128]{2,1,0:T(8,128)S(1)}, u32[]{:S(2)}, u32[]{:S(2)}) %collective-permute-start.13) | collective-permute-done | bytes 98336 | tf_op jit(solution)/shard_map/ppermute | solution.py:39
  82.1 2.1 %collective-permute-start.14 = (f32[2,48,128]{2,1,0:T(8,128)S(1)}, f32[2,48,128]{2,1,0:T(8,128)S(1)}, u32[]{:S(2)}, u32[]{:S(2)}) collective-permute-start(f32[2,48,128]{2,1,0:T(8,128)S(1)} %slice.63), channel_id=1, source_target_pairs={{0,24},{8,16},{16,8},{24,0},{32,56},{40,48},{48,40},{56,32},{64,88... | collective-permute-start | bytes 147464 | tf_op jit(solution)/shard_map/ppermute | solution.py:39
  84.2 3.9 %collective-permute-done.14 = f32[2,48,128]{2,1,0:T(8,128)S(1)} collective-permute-done((f32[2,48,128]{2,1,0:T(8,128)S(1)}, f32[2,48,128]{2,1,0:T(8,128)S(1)}, u32[]{:S(2)}, u32[]{:S(2)}) %collective-permute-start.14) | collective-permute-done | bytes 49184 | tf_op jit(solution)/shard_map/ppermute | solution.py:39
  88.1 3.3 %collective-permute-start.15 = (f32[1,48,128]{2,1,0:T(8,128)S(1)}, f32[1,48,128]{2,1,0:T(8,128)S(1)}, u32[]{:S(2)}, u32[]{:S(2)}) collective-permute-start(f32[1,48,128]{2,1,0:T(8,128)S(1)} %slice.65), channel_id=1, source_target_pairs={{0,56},{8,48},{16,40},{24,32},{32,24},{40,16},{48,8},{56,0},{64,12... | collective-permute-start | bytes 73736 | tf_op jit(solution)/shard_map/ppermute | solution.py:39
  91.4 1.8 %collective-permute-done.15 = f32[1,48,128]{2,1,0:T(8,128)S(1)} collective-permute-done((f32[1,48,128]{2,1,0:T(8,128)S(1)}, f32[1,48,128]{2,1,0:T(8,128)S(1)}, u32[]{:S(2)}, u32[]{:S(2)}) %collective-permute-start.15) | collective-permute-done | bytes 24608 | tf_op jit(solution)/shard_map/ppermute | solution.py:39
  93.2 0.6 fusion
  (27 shorter events, 0.2 us)
Async XLA Ops:
  0.0 15.8 %copy-start.4 = (s32[1024,48]{0,1:T(8,128)S(1)}, s32[1024,48]{0,1:T(8,128)}, u32[]{:S(2)}) copy-start(s32[1024,48]{0,1:T(8,128)} %param.8) | copy-start | bytes 589828
  0.0 16.0 %copy-start.3 = (s32[1024]{0:T(1024)S(1)}, s32[1024]{0:T(1024)}, u32[]{:S(2)}) copy-start(s32[1024]{0:T(1024)} %param.9) | copy-start | bytes 12292
  0.0 16.0 %copy-start.2 = (s32[1024]{0:T(1024)S(1)}, s32[1024]{0:T(1024)}, u32[]{:S(2)}) copy-start(s32[1024]{0:T(1024)} %param.7) | copy-start | bytes 12292
  1.7 3.4 %copy-start = (bf16[1024,4096]{1,0:T(8,128)(2,1)S(1)}, bf16[1024,4096]{1,0:T(8,128)(2,1)}, u32[]{:S(2)}) copy-start(bf16[1024,4096]{1,0:T(8,128)(2,1)} %geno_ref.5) | copy-start | bytes 25165828
  8.7 1.4 %collective-permute-start = (f32[4,6,1024]{2,1,0:T(8,128)S(1)}, f32[4,6,1024]{2,1,0:T(8,128)S(1)}, u32[]{:S(2)}, u32[]{:S(2)}) collective-permute-start(f32[4,6,1024]{2,1,0:T(8,128)S(1)} %slice.54), channel_id=1, source_target_pairs={{0,1},{1,0},{2,3},{3,2},{4,5},{5,4},{6,7},{7,6},{8,9},{9,8},{10,11... | collective-permute-start | bytes 294920 | tf_op jit(solution)/shard_map/ppermute | solution.py:39
  10.1 5.6 %collective-permute-start.1 = (f32[2,6,1024]{2,1,0:T(8,128)S(1)}, f32[2,6,1024]{2,1,0:T(8,128)S(1)}, u32[]{:S(2)}, u32[]{:S(2)}) collective-permute-start(f32[2,6,1024]{2,1,0:T(8,128)S(1)} %slice.56), channel_id=1, source_target_pairs={{0,6},{1,7},{2,4},{3,5},{4,2},{5,3},{6,0},{7,1},{8,14},{9,15},{10,... | collective-permute-start | bytes 147464 | tf_op jit(solution)/shard_map/ppermute | solution.py:39
  15.7 4.0 %collective-permute-start.2 = (f32[1,6,1024]{2,1,0:T(8,128)S(1)}, f32[1,6,1024]{2,1,0:T(8,128)S(1)}, u32[]{:S(2)}, u32[]{:S(2)}) collective-permute-start(f32[1,6,1024]{2,1,0:T(8,128)S(1)} %slice.57), channel_id=1, source_target_pairs={{0,2},{1,3},{2,0},{3,1},{4,6},{5,7},{6,4},{7,5},{8,10},{9,11},{10,... | collective-permute-start | bytes 73736 | tf_op jit(solution)/shard_map/ppermute | solution.py:39
  20.5 7.5 %collective-permute-start.3 = (f32[1,6,128]{2,1,0:T(8,128)S(1)}, f32[1,6,128]{2,1,0:T(8,128)S(1)}, u32[]{:S(2)}, u32[]{:S(2)}) collective-permute-start(f32[1,6,128]{2,1,0:T(8,128)S(1)} %get-tuple-element.12), channel_id=1, source_target_pairs={{0,56},{8,48},{16,40},{24,32},{32,24},{40,16},{48,8},{56,0},{64,12... | collective-permute-start | bytes 9224 | tf_op jit(solution)/shard_map/ppermute | solution.py:39
  27.9 5.4 %collective-permute-start.4 = (f32[2,6,128]{2,1,0:T(8,128)S(1)}, f32[2,6,128]{2,1,0:T(8,128)S(1)}, u32[]{:S(2)}, u32[]{:S(2)}) collective-permute-start(f32[2,6,128]{2,1,0:T(8,128)S(1)} %pad_maximum_fusion.4), channel_id=1, source_target_pairs={{0,24},{8,16},{16,8},{24,0},{32,56},{40,48},{48,40},{56,32},{64,88... | collective-permute-start | bytes 18440 | tf_op jit(solution)/shard_map/ppermute | solution.py:39
  33.4 4.9 %collective-permute-start.5 = (f32[4,6,128]{2,1,0:T(8,128)S(1)}, f32[4,6,128]{2,1,0:T(8,128)S(1)}, u32[]{:S(2)}, u32[]{:S(2)}) collective-permute-start(f32[4,6,128]{2,1,0:T(8,128)S(1)} %pad_maximum_fusion.3), channel_id=1, source_target_pairs={{0,192},{8,200},{16,208},{24,216},{32,224},{40,232},{48,240},{56,2... | collective-permute-start | bytes 36872 | tf_op jit(solution)/shard_map/ppermute | solution.py:39
  38.3 3.9 %collective-permute-start.6 = (f32[8,6,128]{2,1,0:T(8,128)S(1)}, f32[8,6,128]{2,1,0:T(8,128)S(1)}, u32[]{:S(2)}, u32[]{:S(2)}) collective-permute-start(f32[8,6,128]{2,1,0:T(8,128)S(1)} %pad_maximum_fusion.1), channel_id=1, source_target_pairs={{0,8},{8,0},{16,24},{24,16},{32,40},{40,32},{48,56},{56,48},{64,72... | collective-permute-start | bytes 73736 | tf_op jit(solution)/shard_map/ppermute | solution.py:39
  42.3 4.3 %collective-permute-start.7 = (f32[16,6,128]{2,1,0:T(8,128)S(1)}, f32[16,6,128]{2,1,0:T(8,128)S(1)}, u32[]{:S(2)}, u32[]{:S(2)}) collective-permute-start(f32[16,6,128]{2,1,0:T(8,128)S(1)} %constant_dynamic-update-slice_fusion.near_ref), channel_id=1, source_target_pairs={{0,64},{8,72},{16,80},{24,88},{32,96},{40,104},{48,112},{56,120},{... | collective-permute-start | bytes 147464 | tf_op jit(solution)/shard_map/ppermute | solution.py:39
  48.3 3.8 %collective-permute-start.8 = (bf16[1,6,1024]{2,1,0:T(8,128)(2,1)S(1)}, bf16[1,6,1024]{2,1,0:T(8,128)(2,1)S(1)}, u32[]{:S(2)}, u32[]{:S(2)}) collective-permute-start(bf16[1,6,1024]{2,1,0:T(8,128)(2,1)S(1)} %shard_map.58), channel_id=1, source_target_pairs={{0,2},{1,3},{2,0},{3,1},{4,6},{5,7},{6,4},{7,5},{8,10},{9,11},{10,... | collective-permute-start | bytes 36872 | tf_op jit(solution)/shard_map/ppermute | solution.py:39
  52.1 5.2 %collective-permute-start.9 = (bf16[2,6,1024]{2,1,0:T(8,128)(2,1)S(1)}, bf16[2,6,1024]{2,1,0:T(8,128)(2,1)S(1)}, u32[]{:S(2)}, u32[]{:S(2)}) collective-permute-start(bf16[2,6,1024]{2,1,0:T(8,128)(2,1)S(1)} %pad_maximum_fusion.2), channel_id=1, source_target_pairs={{0,6},{1,7},{2,4},{3,5},{4,2},{5,3},{6,0},{7,1},{8,14},{9,15},{10,... | collective-permute-start | bytes 73736 | tf_op jit(solution)/shard_map/ppermute | solution.py:39
  57.3 1.3 %collective-permute-start.10 = (bf16[4,6,1024]{2,1,0:T(8,128)(2,1)S(1)}, bf16[4,6,1024]{2,1,0:T(8,128)(2,1)S(1)}, u32[]{:S(2)}, u32[]{:S(2)}) collective-permute-start(bf16[4,6,1024]{2,1,0:T(8,128)(2,1)S(1)} %pad_maximum_fusion.near_ref), channel_id=1, source_target_pairs={{0,1},{1,0},{2,3},{3,2},{4,5},{5,4},{6,7},{7,6},{8,9},{9,8},{10,11... | collective-permute-start | bytes 147464 | tf_op jit(solution)/shard_map/ppermute | solution.py:39
  58.7 3.4 %copy-start.1 = (bf16[1024,4096]{1,0:T(8,128)(2,1)S(1)}, bf16[1024,4096]{1,0:T(8,128)(2,1)}, u32[]{:S(2)}) copy-start(bf16[1024,4096]{1,0:T(8,128)(2,1)} %geno_ref.5) | copy-start | bytes 25165828
  64.3 7.1 %collective-permute-start.11 = (bf16[16,48,128]{2,1,0:T(8,128)(2,1)S(1)}, bf16[16,48,128]{2,1,0:T(8,128)(2,1)S(1)}, u32[]{:S(2)}, u32[]{:S(2)}) collective-permute-start(bf16[16,48,128]{2,1,0:T(8,128)(2,1)S(1)} %shard_map.60), channel_id=1, source_target_pairs={{0,64},{8,72},{16,80},{24,88},{32,96},{40,104},{48,112},{56,120},{... | collective-permute-start | bytes 589832 | tf_op jit(solution)/shard_map/ppermute | solution.py:39
  71.4 4.7 %collective-permute-start.12 = (bf16[8,48,128]{2,1,0:T(8,128)(2,1)S(1)}, bf16[8,48,128]{2,1,0:T(8,128)(2,1)S(1)}, u32[]{:S(2)}, u32[]{:S(2)}) collective-permute-start(bf16[8,48,128]{2,1,0:T(8,128)(2,1)S(1)} %slice.75), channel_id=1, source_target_pairs={{0,8},{8,0},{16,24},{24,16},{32,40},{40,32},{48,56},{56,48},{64,72... | collective-permute-start | bytes 294920 | tf_op jit(solution)/shard_map/ppermute | solution.py:39
  76.2 5.9 %collective-permute-start.13 = (f32[4,48,128]{2,1,0:T(8,128)S(1)}, f32[4,48,128]{2,1,0:T(8,128)S(1)}, u32[]{:S(2)}, u32[]{:S(2)}) collective-permute-start(f32[4,48,128]{2,1,0:T(8,128)S(1)} %slice.61), channel_id=1, source_target_pairs={{0,192},{8,200},{16,208},{24,216},{32,224},{40,232},{48,240},{56,2... | collective-permute-start | bytes 294920 | tf_op jit(solution)/shard_map/ppermute | solution.py:39
  82.1 6.0 %collective-permute-start.14 = (f32[2,48,128]{2,1,0:T(8,128)S(1)}, f32[2,48,128]{2,1,0:T(8,128)S(1)}, u32[]{:S(2)}, u32[]{:S(2)}) collective-permute-start(f32[2,48,128]{2,1,0:T(8,128)S(1)} %slice.63), channel_id=1, source_target_pairs={{0,24},{8,16},{16,8},{24,0},{32,56},{40,48},{48,40},{56,32},{64,88... | collective-permute-start | bytes 147464 | tf_op jit(solution)/shard_map/ppermute | solution.py:39
  88.1 5.1 %collective-permute-start.15 = (f32[1,48,128]{2,1,0:T(8,128)S(1)}, f32[1,48,128]{2,1,0:T(8,128)S(1)}, u32[]{:S(2)}, u32[]{:S(2)}) collective-permute-start(f32[1,48,128]{2,1,0:T(8,128)S(1)} %slice.65), channel_id=1, source_target_pairs={{0,56},{8,48},{16,40},{24,32},{32,24},{40,16},{48,8},{56,0},{64,12... | collective-permute-start | bytes 73736 | tf_op jit(solution)/shard_map/ppermute | solution.py:39

commit v2 on v0

v2 whole, which is shorter than its diff:
```python
import functools

import jax
import jax.numpy as jnp
from jax import lax
from jax.experimental import pallas as pl
from jax.experimental.pallas import tpu as pltpu
from jax.sharding import PartitionSpec as P

COLS = 48
HALF = 24
ROWS = 1024
SLOTS = 64
COUNT = 32
MIB = 1024 * 1024
SCALE = 0.125


def parts3(value):
    high = value.astype(jnp.bfloat16)
    rest = value - high.astype(jnp.float32)
    mid = rest.astype(jnp.bfloat16)
    low = (rest - mid.astype(jnp.float32)).astype(jnp.bfloat16)
    return high, mid, low


def smem():
    return pl.BlockSpec(memory_space=pltpu.SMEM)


def vmem():
    return pl.BlockSpec(memory_space=pltpu.VMEM)


def eta_kernel(where_ref, geno_ref, coefs_ref, out_ref):
    core = where_ref[0]
    block = lax.dot_general(
        coefs_ref[...], geno_ref[...], (((1,), (1,)), ((), ())), preferred_element_type=jnp.float32
    )
    out_ref[core] = block[:HALF]
    out_ref[1 - core] = block[HALF:]


def eta_halves(where, genotype, coefs):
    rows, depth = genotype.shape
    block = 256
    return pl.pallas_call(
        eta_kernel,
        grid_spec=pltpu.PrefetchScalarGridSpec(
            num_scalar_prefetch=1,
            grid=(rows // block,),
            in_specs=[
                pl.BlockSpec((block, depth), lambda i, w: (i, 0)),
                pl.BlockSpec((COLS, depth), lambda i, w: (0, 0)),
            ],
            out_specs=pl.BlockSpec((2, HALF, block), lambda i, w: (0, 0, i)),
        ),
        out_shape=jax.ShapeDtypeStruct((2, HALF, rows), jnp.float32),
        compiler_params=pltpu.CompilerParams(vmem_limit_bytes=56 * MIB),
        cost_estimate=pl.CostEstimate(
            flops=2 * rows * depth * 128, bytes_accessed=rows * depth * 2, transcendentals=0
        ),
    )(where, genotype, coefs)


def weight_kernel(where_ref, eta_ref, folds_ref, events_ref, groups_ref, weight_ref, counted_ref, pack_ref):
    core = where_ref[0]
    base = where_ref[1] * (SLOTS - 1)
    fold = folds_ref[pl.ds(pl.multiple_of(core * HALF, 8), HALF), :].astype(jnp.float32)
    weight = fold * jnp.exp(eta_ref[...])
    counted = fold * events_ref[...].astype(jnp.float32)
    weight_ref[...] = weight
    counted_ref[...] = counted
    slot = lax.broadcasted_iota(jnp.int32, (SLOTS, ROWS), 0)
    hot = (slot == groups_ref[...] - base).astype(jnp.bfloat16)

    def total(part):
        return lax.dot_general(
            part, hot, (((1,), (1,)), ((), ())), preferred_element_type=jnp.float32
        )

    high, mid, low = parts3(weight)
    sums = total(high) + (total(mid) + total(low))
    pack = jnp.concatenate([sums, total(counted.astype(jnp.bfloat16))], axis=1).astype(jnp.bfloat16)
    for device in range(COUNT):
        pack_ref[device] = pack


def weights(where, eta, folds, events, groups):
    return pl.pallas_call(
        weight_kernel,
        in_specs=[smem()] + [vmem()] * 4,
        out_specs=[vmem()] * 3,
        out_shape=[
            jax.ShapeDtypeStruct((HALF, ROWS), jnp.float32),
            jax.ShapeDtypeStruct((HALF, ROWS), jnp.float32),
            jax.ShapeDtypeStruct((COUNT, HALF, 2 * SLOTS), jnp.bfloat16),
        ],
        compiler_params=pltpu.CompilerParams(vmem_limit_bytes=16 * MIB),
        cost_estimate=pl.CostEstimate(flops=10**8, bytes_accessed=10**6, transcendentals=0),
    )(where, eta, folds, events, groups)


def resid_kernel(where_ref, pack_ref, weight_ref, counted_ref, groups_ref, resid_ref):
    mine = where_ref[1]
    base = mine * (SLOTS - 1)
    wide = 2 * SLOTS
    source = lax.broadcasted_iota(jnp.int32, (wide, 3 * wide), 0)
    target = lax.broadcasted_iota(jnp.int32, (wide, 3 * wide), 1)
    suffix_part = (target < SLOTS) & (source >= target) & (source < SLOTS)
    total_part = (target >= wide) & (target < 2 * wide) & (source < SLOTS)
    count_part = (target >= 2 * wide) & (source - SLOTS == target - 2 * wide)
    matrix = jnp.where(suffix_part | total_part | count_part, 1.0, 0.0).astype(jnp.bfloat16)
    flat = pack_ref[...].astype(jnp.float32).reshape(COUNT * HALF, wide).astype(jnp.bfloat16)
    sums = jnp.dot(flat, matrix, preferred_element_type=jnp.float32)
    zero = jnp.zeros((HALF, wide), jnp.float32)
    after, before, own = zero, zero, zero
    for device in reversed(range(COUNT)):
        part = sums[device * HALF : device * HALF + HALF]
        count = part[:, 2 * wide :]
        some = count > 0
        risk = jnp.where(some, part[:, :wide] + after, 1.0)
        added = jnp.where(some, count / risk, 0.0)
        after = after + part[:, wide : 2 * wide]
        before = before + jnp.where(device < mine, added, 0.0)
        own = own + jnp.where(device == mine, added, 0.0)
    slot = lax.broadcasted_iota(jnp.int32, (wide, ROWS), 0)
    upto = (slot <= groups_ref[...] - base).astype(jnp.bfloat16)
    high, mid, low = parts3(own)
    hazard = jnp.dot(high, upto, preferred_element_type=jnp.float32) + (
        jnp.dot(mid, upto, preferred_element_type=jnp.float32)
        + jnp.dot(low, upto, preferred_element_type=jnp.float32)
    )
    hazard = hazard + jnp.sum(before, axis=1, keepdims=True)
    resid = counted_ref[...] - weight_ref[...] * hazard
    resid_ref[...] = resid.astype(jnp.bfloat16)


def residuals(where, pack, weight, counted, groups):
    return pl.pallas_call(
        resid_kernel,
        in_specs=[smem()] + [vmem()] * 4,
        out_specs=vmem(),
        out_shape=jax.ShapeDtypeStruct((HALF, ROWS), jnp.bfloat16),
        compiler_params=pltpu.CompilerParams(vmem_limit_bytes=16 * MIB),
        cost_estimate=pl.CostEstimate(flops=10**8, bytes_accessed=10**6, transcendentals=0),
    )(where, pack, weight, counted, groups)


def grad_kernel(where_ref, geno_ref, own_ref, other_ref, out_ref, turned):
    @pl.when(pl.program_id(0) == 0)
    def _():
        first = where_ref[0] == 0
        own = own_ref[...].astype(jnp.float32)
        other = other_ref[...].astype(jnp.float32)
        both = jnp.concatenate(
            [jnp.where(first, own, other), jnp.where(first, other, own)], axis=0
        )
        turned[...] = both.astype(jnp.bfloat16)

    block = jnp.dot(turned[...], geno_ref[...], preferred_element_type=jnp.float32) * SCALE
    for piece in range(geno_ref.shape[1] // 128):
        out_ref[piece] = block[:, 128 * piece : 128 * piece + 128].astype(out_ref.dtype)


def grad_slots(dtype, where, genotype, own, other):
    rows, depth = genotype.shape
    block = 512
    return pl.pallas_call(
        grad_kernel,
        grid_spec=pltpu.PrefetchScalarGridSpec(
            num_scalar_prefetch=1,
            grid=(depth // block,),
            in_specs=[
                pl.BlockSpec((rows, block), lambda i, w: (0, i)),
                pl.BlockSpec((HALF, rows), lambda i, w: (0, 0)),
                pl.BlockSpec((HALF, rows), lambda i, w: (0, 0)),
            ],
            out_specs=pl.BlockSpec((block // 128, COLS, 128), lambda i, w: (i, 0, 0)),
            scratch_shapes=[pltpu.VMEM((COLS, rows), jnp.bfloat16)],
        ),
        out_shape=jax.ShapeDtypeStruct((depth // 128, COLS, 128), dtype),
        compiler_params=pltpu.CompilerParams(vmem_limit_bytes=32 * MIB),
        cost_estimate=pl.CostEstimate(
            flops=2 * rows * depth * 128, bytes_accessed=rows * depth * 2, transcendentals=0
        ),
    )(where, genotype, own, other)


def swap(value, mask):
    return lax.ppermute(value, "var", [(index, index ^ mask) for index in range(8)])


def per_device(genotype, coefs, events, folds, groups):
    subj = lax.axis_index("subj")
    var = lax.axis_index("var")
    where = jnp.stack([var & 1, subj]).astype(jnp.int32)
    events = events.reshape(1, ROWS)
    groups = groups.reshape(1, ROWS)

    eta = eta_halves(where, genotype, coefs.T)
    eta = eta[0] + swap(eta[1], 1)
    sent = eta.astype(jnp.float16)
    for mask in (2, 4, 6):
        eta = eta + swap(sent, mask).astype(jnp.float32)
    weight, counted, pack = weights(where, eta, folds.T, events, groups)
    pack = lax.all_to_all(pack, "subj", 0, 0)
    own = residuals(where, pack, weight, counted, groups)
    other = swap(own, 1)
    slots = grad_slots(jnp.float32, where, genotype, own, other).astype(jnp.float16)
    slots = lax.all_to_all(slots, "subj", 0, 0)
    factor = -1.0 / (SCALE * float(COUNT * ROWS) ** 0.5)
    return (jnp.sum(slots.astype(jnp.float32), axis=0) * factor).T


def solution(mesh):
    in_specs = (P("subj", "var"), P("var", None), P("subj"), P("subj", None), P("subj"))
    out_specs = P(("var", "subj"), None)
    return jax.shard_map(
        per_device, mesh=mesh, in_specs=in_specs, out_specs=out_specs, check_vma=False
    )
```

time: 407 us -> 73 us (0.18)
  waiting for transfers between devices: 259 us -> 6.77 us
  blocking collectives: 75.6 us -> 41.1 us
  other arithmetic: 32.5 us -> 3.15 us
  between operations: 14.9 us -> 0.1 us
  Pallas kernels: 0 us -> 13 us
  matrix products: 12.6 us -> 0 us
  local copies, waits for them, and re-layouts: 9.9 us -> 4.3 us
  starting transfers between devices: 0.08 us -> 4.28 us
    reduce_scatter x1 -> x0, waiting for transfers between devices: 197 us -> none  [per_device(): lax.psum_scatter(product * factor, 'subj', scatter_dimension=0, tiled=True)]
    all_gather x2 -> x0, blocking collectives: 75.6 us -> none  [carried_in(): pieces = lax.all_gather(value, axis)]
    psum x1 -> x0, waiting for transfers between devices: 62.1 us -> none  [per_device(): eta = lax.psum(partial_eta, 'var')]
    all_to_all x0 -> x2, blocking collectives: none -> 41.1 us  [the longest x1 21.6 us: per_device(): pack = lax.all_to_all(pack, 'subj', 0, 0)]
    another operation x11 -> x1, other arithmetic: 30.1 us -> 0.59 us  [per_device(): where = jnp.stack([var & 1, subj]).astype(jnp.int32)]
    pallas_call x0 -> x4, Pallas kernels: none -> 13 us  [the longest x1 7.09 us: eta_halves(): pl.pallas_call(eta_kernel, grid_spec=pltpu.PrefetchScalarGridSpec(num_sca...]
    dot_general x2 -> x0, matrix products: 12.6 us -> none  [the longest x1 6.69 us: per_device(): partial_eta = jnp.dot(genotype, coefs, preferred_element_type=jnp.float32)]
    ppermute x0 -> x5, waiting for transfers between devices: none -> 6.77 us  [swap(): lax.ppermute(value, 'var', [(index, index ^ mask) for index in range(8)])]
  transfers between devices with their start and end apart: 2 -> 5, of which waited for: 2 -> 4; matrix products, arithmetic and copies ran while one was open for 1% -> 0% of each run, Pallas kernels for 0% -> 0%
where the time goes in v2:
time: 73 us; the launch traced here: 72.7 us
  blocking collectives  41.1 us (56%)
  Pallas kernels  13 us (18%)
  waiting for transfers between devices  6.77 us (9%)
  local copies, waits for them, and re-layouts  4.3 us (6%)
  starting transfers between devices  4.28 us (6%)
  other arithmetic  3.15 us (4%)
    all_to_all x1, blocking collectives, per_device(): pack = lax.all_to_all(pack, 'subj', 0, 0)  21.6 us
    all_to_all x1, blocking collectives, per_device(): slots = lax.all_to_all(slots, 'subj', 0, 0)  19.5 us
    pallas_call x1, Pallas kernels, eta_halves(): pl.pallas_call(eta_kernel, grid_spec=pltpu.PrefetchScalarGridSpec(num_sca...  7.09 us
    ppermute x5, waiting for transfers between devices, swap(): lax.ppermute(value, 'var', [(index, index ^ mask) for index in range(8)])  6.77 us
    ppermute x5, starting transfers between devices, swap(): lax.ppermute(value, 'var', [(index, index ^ mask) for index in range(8)])  4.28 us
    pallas_call x1, Pallas kernels, grad_slots(): pl.pallas_call(grad_kernel, grid_spec=pltpu.PrefetchScalarGridSpec(num_sc...  3.64 us
    unnamed x10, local copies, waits for them, and re-layouts  3.4 us
  transfers between devices with their start and end apart: 5, of which 4 were waited for; matrix products, arithmetic and copies ran while one was open for 0% of the time, Pallas kernels for 0%

profile of v2, /device:TPU:32, one launch (start us, length us, event | category | flops | bytes accessed | tf_op | source)
XLA Modules:
  0.0 72.7 jit_solution(7215850274576847697)
XLA Ops:
  0.0 0.0 copy-start.2
  0.0 0.0 copy-start.3
  0.0 0.0 copy-start.4
  0.0 0.6 pad_add_fusion.where_ref
  0.6 0.0 copy-start.1
  0.6 7.1 %shard_map.55 = f32[2,24,1024]{2,1,0:T(8,128)} custom-call(s32[2]{0:T(128)} %pad_add_fusion.where_ref, bf16[1024,4096]{1,0:T(8,128)(2,1)} %geno_ref.3, bf16[48,4096]{1,0:T(8,128)(2,1)} %bitcast.22), custom_call_target="tpu_custom_call" | custom-call | flops 1073741824 | bytes 8388608 | tf_op jit(solution)/shard_map/pallas_call | solution.py:47
  7.7 0.9 %slice_bitcast_fusion = f32[24,1024]{1,0:T(8,128)S(1)} fusion(f32[2,24,1024]{2,1,0:T(8,128)} %shard_map.55), kind=kLoop, calls=%fused_computation.1 | loop fusion | bytes 196608 | tf_op jit(solution)/shard_map/squeeze | solution.py:202
  8.6 0.0 collective-permute-start
  8.6 1.3 %collective-permute-done = f32[24,1024]{1,0:T(8,128)S(1)} collective-permute-done((f32[24,1024]{1,0:T(8,128)S(1)}, f32[24,1024]{1,0:T(8,128)S(1)}, u32[]{:S(2)}, u32[]{:S(2)}) %collective-permute-start) | collective-permute-done | bytes 98336 | tf_op jit(solution)/shard_map/ppermute | solution.py:191
  9.9 0.9 %fusion.1 = f16[24,1024]{1,0:T(8,128)(2,1)S(1)} fusion(f32[24,1024]{1,0:T(8,128)S(1)} %collective-permute-done, f32[2,24,1024]{2,1,0:T(8,128)} %shard_map.55), kind=kLoop, calls=%fused_computation.5 | loop fusion | flops 49152 | bytes 245760 | tf_op jit(solution)/shard_map/convert_element_type | solution.py:203
  10.8 2.8 %collective-permute-start.3 = (f16[24,1024]{1,0:T(8,128)(2,1)S(1)}, f16[24,1024]{1,0:T(8,128)(2,1)S(1)}, u32[]{:S(2)}, u32[]{:S(2)}) collective-permute-start(f16[24,1024]{1,0:T(8,128)(2,1)S(1)} %fusion.1), channel_id=1, source_target_pairs={{0,6},{1,7},{2,4},{3,5},{4,2},{5,3},{6,0},{7,1},{8,14},{9,15},{10,... | collective-permute-start | bytes 147464 | tf_op jit(solution)/shard_map/ppermute | solution.py:191
  13.7 0.8 %collective-permute-start.2 = (f16[24,1024]{1,0:T(8,128)(2,1)S(1)}, f16[24,1024]{1,0:T(8,128)(2,1)S(1)}, u32[]{:S(2)}, u32[]{:S(2)}) collective-permute-start(f16[24,1024]{1,0:T(8,128)(2,1)S(1)} %fusion.1), channel_id=1, source_target_pairs={{0,4},{1,5},{2,6},{3,7},{4,0},{5,1},{6,2},{7,3},{8,12},{9,13},{10,... | collective-permute-start | bytes 147464 | tf_op jit(solution)/shard_map/ppermute | solution.py:191
  14.5 0.5 collective-permute-start.1
  15.0 1.2 %collective-permute-done.3 = f16[24,1024]{1,0:T(8,128)(2,1)S(1)} collective-permute-done((f16[24,1024]{1,0:T(8,128)(2,1)S(1)}, f16[24,1024]{1,0:T(8,128)(2,1)S(1)}, u32[]{:S(2)}, u32[]{:S(2)}) %collective-permute-start.3) | collective-permute-done | bytes 49184 | tf_op jit(solution)/shard_map/ppermute | solution.py:191
  16.2 3.1 %collective-permute-done.2 = f16[24,1024]{1,0:T(8,128)(2,1)S(1)} collective-permute-done((f16[24,1024]{1,0:T(8,128)(2,1)S(1)}, f16[24,1024]{1,0:T(8,128)(2,1)S(1)}, u32[]{:S(2)}, u32[]{:S(2)}) %collective-permute-start.2) | collective-permute-done | bytes 49184 | tf_op jit(solution)/shard_map/ppermute | solution.py:191
  19.2 0.0 collective-permute-done.1
  19.3 0.9 %convert_add_fusion.eta_ref = f32[24,1024]{1,0:T(8,128)S(1)} fusion(f16[24,1024]{1,0:T(8,128)(2,1)S(1)} %collective-permute-done.3, f16[24,1024]{1,0:T(8,128)(2,1)S(1)} %collective-permute-done.2, f16[24,1024]{1,0:T(8,128)(2,1)S(1)} %collective-permute-done.1, f32[24,1024]{1,0:T(8,128)S(1)} %collective-permute-done, f32[2,24,1024]{2,1,0:T(8,128)} %shard_map.55), kind=kLoop, calls=%fused_computation.4 | loop fusion | flops 172032 | bytes 442368 | tf_op jit(solution)/shard_map/add | solution.py:205
  20.2 0.0 copy-done.2
  20.2 0.0 copy-done.3
  20.2 0.0 copy-done.4
  20.2 0.0 copy-done.1
  20.2 0.9 %shard_map.56 = (f32[24,1024]{1,0:T(8,128)S(1)}, f32[24,1024]{1,0:T(8,128)S(1)}, bf16[32,24,128]{2,1,0:T(8,128)(2,1)S(1)}) custom-call(s32[2]{0:T(128)S(1)} %copy-done.1, f32[24,1024]{1,0:T(8,128)S(1)} %convert_add_fusion.eta_ref, s32[48,1024]{1,0:T(8,128)S(1)} %bitcast.20, s32[1,1024]{1,0:T(1,128)S(1)} %bitcast.21, s32[1,1024]{1,0:T(1,128)S(1)} %bitcast.18), custom_call_target="tpu_custom_call" | custom-call | flops 100000000 | bytes 1000000 | tf_op jit(solution)/shard_map/pallas_call | solution.py:90
  21.1 21.6 %all_to_all.10.pack_ref = bf16[32,24,128]{2,1,0:T(8,128)(2,1)S(1)} all-to-all(bf16[32,24,128]{2,1,0:T(8,128)(2,1)S(1)} %get-tuple-element.8), channel_id=1, replica_groups=mesh['subj'=32,'var'=8] {'subj'}, dimensions={0} | all-to-all | bytes 393216 | tf_op jit(solution)/shard_map/all_to_all | solution.py:207
  42.7 1.4 %shard_map.57.own_ref = bf16[24,1024]{1,0:T(8,128)(2,1)S(1)} custom-call(s32[2]{0:T(128)S(1)} %copy-done.1, bf16[32,24,128]{2,1,0:T(8,128)(2,1)S(1)} %all_to_all.10.pack_ref, f32[24,1024]{1,0:T(8,128)S(1)} %get-tuple-element.9.weight_ref, f32[24,1024]{1,0:T(8,128)S(1)} %get-tuple-element.10.counted_ref, s32[1,1024]{1,0:T(1,128)S(1)} %bitcast.19), custom_call_target="tpu_custom_call" | custom-call | flops 100000000 | bytes 1000000 | tf_op jit(solution)/shard_map/pallas_call | solution.py:140
  44.1 0.1 collective-permute-start.4
  44.2 1.2 %collective-permute-done.4.other_ref = bf16[24,1024]{1,0:T(8,128)(2,1)S(1)} collective-permute-done((bf16[24,1024]{1,0:T(8,128)(2,1)S(1)}, bf16[24,1024]{1,0:T(8,128)(2,1)S(1)}, u32[]{:S(2)}, u32[]{:S(2)}) %collective-permute-start.4) | collective-permute-done | bytes 49184 | tf_op jit(solution)/shard_map/ppermute | solution.py:191
  45.4 0.0 copy-start
  45.4 3.4 %copy-done = bf16[1024,4096]{1,0:T(8,128)(2,1)S(1)} copy-done((bf16[1024,4096]{1,0:T(8,128)(2,1)S(1)}, bf16[1024,4096]{1,0:T(8,128)(2,1)}, u32[]{:S(2)}) %copy-start) | copy-done | bytes 8388632
  48.8 3.6 %shard_map.58 = f32[32,48,128]{2,1,0:T(8,128)S(1)} custom-call(s32[2]{0:T(128)S(1)} %copy-done.1, bf16[1024,4096]{1,0:T(8,128)(2,1)S(1)} %copy-done, bf16[24,1024]{1,0:T(8,128)(2,1)S(1)} %shard_map.57.own_ref, bf16[24,1024]{1,0:T(8,128)(2,1)S(1)} %collective-permute-done.4.other_ref), custom_call_target="tpu_custom_call" | custom-call | flops 1073741824 | bytes 8388608 | tf_op jit(solution)/shard_map/pallas_call | solution.py:169
  52.5 0.1 convert_element_type.22
  52.5 19.5 %all_to_all.11 = f16[32,48,128]{2,1,0:T(8,128)(2,1)S(1)} all-to-all(f16[32,48,128]{2,1,0:T(8,128)(2,1)S(1)} %convert_element_type.22), channel_id=1, replica_groups=mesh['subj'=32,'var'=8] {'subj'}, dimensions={0} | all-to-all | bytes 786432 | tf_op jit(solution)/shard_map/all_to_all | solution.py:211
  72.0 0.1 convert_reduce_fusion
  72.1 0.6 multiply_bitcast_fusion
Async XLA Ops:
  0.0 20.2 %copy-start.2 = (s32[1024]{0:T(1024)S(1)}, s32[1024]{0:T(1024)}, u32[]{:S(2)}) copy-start(s32[1024]{0:T(1024)} %param.9) | copy-start | bytes 12292
  0.0 20.2 %copy-start.3 = (s32[1024,48]{0,1:T(8,128)S(1)}, s32[1024,48]{0,1:T(8,128)}, u32[]{:S(2)}) copy-start(s32[1024,48]{0,1:T(8,128)} %param.8) | copy-start | bytes 589828
  0.0 20.2 %copy-start.4 = (s32[1024]{0:T(1024)S(1)}, s32[1024]{0:T(1024)}, u32[]{:S(2)}) copy-start(s32[1024]{0:T(1024)} %param.7) | copy-start | bytes 12292
  0.6 19.6 %copy-start.1 = (s32[2]{0:T(128)S(1)}, s32[2]{0:T(128)}, u32[]{:S(2)}) copy-start(s32[2]{0:T(128)} %pad_add_fusion.where_ref) | copy-start | bytes 28
  8.6 1.3 %collective-permute-start = (f32[24,1024]{1,0:T(8,128)S(1)}, f32[24,1024]{1,0:T(8,128)S(1)}, u32[]{:S(2)}, u32[]{:S(2)}) collective-permute-start(f32[24,1024]{1,0:T(8,128)S(1)} %slice_bitcast_fusion), channel_id=1, source_target_pairs={{0,1},{1,0},{2,3},{3,2},{4,5},{5,4},{6,7},{7,6},{8,9},{9,8},{10,11... | collective-permute-start | bytes 294920 | tf_op jit(solution)/shard_map/ppermute | solution.py:191
  10.8 5.4 %collective-permute-start.3 = (f16[24,1024]{1,0:T(8,128)(2,1)S(1)}, f16[24,1024]{1,0:T(8,128)(2,1)S(1)}, u32[]{:S(2)}, u32[]{:S(2)}) collective-permute-start(f16[24,1024]{1,0:T(8,128)(2,1)S(1)} %fusion.1), channel_id=1, source_target_pairs={{0,6},{1,7},{2,4},{3,5},{4,2},{5,3},{6,0},{7,1},{8,14},{9,15},{10,... | collective-permute-start | bytes 147464 | tf_op jit(solution)/shard_map/ppermute | solution.py:191
  13.7 5.6 %collective-permute-start.2 = (f16[24,1024]{1,0:T(8,128)(2,1)S(1)}, f16[24,1024]{1,0:T(8,128)(2,1)S(1)}, u32[]{:S(2)}, u32[]{:S(2)}) collective-permute-start(f16[24,1024]{1,0:T(8,128)(2,1)S(1)} %fusion.1), channel_id=1, source_target_pairs={{0,4},{1,5},{2,6},{3,7},{4,0},{5,1},{6,2},{7,3},{8,12},{9,13},{10,... | collective-permute-start | bytes 147464 | tf_op jit(solution)/shard_map/ppermute | solution.py:191
  14.5 4.8 %collective-permute-start.1 = (f16[24,1024]{1,0:T(8,128)(2,1)S(1)}, f16[24,1024]{1,0:T(8,128)(2,1)S(1)}, u32[]{:S(2)}, u32[]{:S(2)}) collective-permute-start(f16[24,1024]{1,0:T(8,128)(2,1)S(1)} %fusion.1), channel_id=1, source_target_pairs={{0,2},{1,3},{2,0},{3,1},{4,6},{5,7},{6,4},{7,5},{8,10},{9,11},{10,... | collective-permute-start | bytes 147464 | tf_op jit(solution)/shard_map/ppermute | solution.py:191
  44.1 1.3 %collective-permute-start.4 = (bf16[24,1024]{1,0:T(8,128)(2,1)S(1)}, bf16[24,1024]{1,0:T(8,128)(2,1)S(1)}, u32[]{:S(2)}, u32[]{:S(2)}) collective-permute-start(bf16[24,1024]{1,0:T(8,128)(2,1)S(1)} %shard_map.57.own_ref), channel_id=1, source_target_pairs={{0,1},{1,0},{2,3},{3,2},{4,5},{5,4},{6,7},{7,6},{8,9},{9,8},{10,11... | collective-permute-start | bytes 147464 | tf_op jit(solution)/shard_map/ppermute | solution.py:191
  45.4 3.4 %copy-start = (bf16[1024,4096]{1,0:T(8,128)(2,1)S(1)}, bf16[1024,4096]{1,0:T(8,128)(2,1)}, u32[]{:S(2)}) copy-start(bf16[1024,4096]{1,0:T(8,128)(2,1)} %geno_ref.3) | copy-start | bytes 25165828

commit v3 on v2

v3 whole, which is shorter than its diff:
```python
import jax
import jax.numpy as jnp
from jax import lax
from jax.experimental import pallas as pl
from jax.experimental.pallas import tpu as pltpu
from jax.sharding import PartitionSpec as P

COLS = 48
HALF = 24
ROWS = 1024
SLOTS = 64
COUNT = 32
MIB = 1024 * 1024
SCALE = 0.125


def parts3(value):
    high = value.astype(jnp.bfloat16)
    rest = value - high.astype(jnp.float32)
    mid = rest.astype(jnp.bfloat16)
    low = (rest - mid.astype(jnp.float32)).astype(jnp.bfloat16)
    return high, mid, low


def vmem():
    return pl.BlockSpec(memory_space=pltpu.VMEM)


def hbm():
    return pl.BlockSpec(memory_space=pltpu.HBM)


def blocks(rows, depth):
    return [(row, 512, at, 512) for row in range(0, rows, 512) for at in range(0, depth, 512)]


def eta_kernel(geno_ref, coefs_ref, out_ref, held_ref, taken, sems, taken_sem):
    core = lax.axis_index("var") & 1
    rows, depth = geno_ref.shape
    pieces = blocks(rows, depth)
    take = pltpu.make_async_copy(coefs_ref, taken, taken_sem)
    take.start()
    copies = []
    for number, (row, high, at, wide) in enumerate(pieces):
        window = (pl.ds(row, high), pl.ds(at, wide))
        copy = pltpu.make_async_copy(geno_ref.at[window], held_ref.at[window], sems.at[number])
        copy.start()
        copies.append(copy)
    take.wait()
    total = None
    for number, (row, high, at, wide) in enumerate(pieces):
        copies[number].wait()
        block = lax.dot_general(
            taken[:, at : at + wide],
            held_ref[row : row + high, at : at + wide],
            (((1,), (1,)), ((), ())),
            preferred_element_type=jnp.float32,
        )
        total = block if at == 0 else total + block
        if at + wide == depth:
            out_ref[core, :, row : row + high] = total[:HALF]
            out_ref[1 - core, :, row : row + high] = total[HALF:]


def eta_halves(genotype, coefs):
    rows, depth = genotype.shape
    return pl.pallas_call(
        eta_kernel,
        in_specs=[hbm(), hbm()],
        out_specs=[vmem(), vmem()],
        out_shape=[
            jax.ShapeDtypeStruct((2, HALF, rows), jnp.float32),
            jax.ShapeDtypeStruct((rows, depth), genotype.dtype),
        ],
        scratch_shapes=[
            pltpu.VMEM((COLS, depth), coefs.dtype),
            pltpu.SemaphoreType.DMA((len(blocks(rows, depth)),)),
            pltpu.SemaphoreType.DMA,
        ],
        compiler_params=pltpu.CompilerParams(vmem_limit_bytes=44 * MIB),
        cost_estimate=pl.CostEstimate(
            flops=2 * rows * depth * 128, bytes_accessed=rows * depth * 2, transcendentals=0
        ),
    )(genotype, coefs)


def weight_kernel(eta_ref, folds_ref, events_ref, groups_ref, weight_ref, counted_ref, pack_ref):
    core = lax.axis_index("var") & 1
    base = lax.axis_index("subj") * (SLOTS - 1)
    fold = folds_ref[pl.ds(pl.multiple_of(core * HALF, 8), HALF), :].astype(jnp.float32)
    weight = fold * jnp.exp(eta_ref[...])
    counted = fold * events_ref[...].astype(jnp.float32)
    weight_ref[...] = weight
    counted_ref[...] = counted
    slot = lax.broadcasted_iota(jnp.int32, (SLOTS, ROWS), 0)
    hot = (slot == groups_ref[...] - base).astype(jnp.bfloat16)

    def total(part):
        return lax.dot_general(
            part, hot, (((1,), (1,)), ((), ())), preferred_element_type=jnp.float32
        )

    high, mid, low = parts3(weight)
    sums = total(high) + (total(mid) + total(low))
    pack = jnp.concatenate([sums, total(counted.astype(jnp.bfloat16))], axis=1).astype(jnp.bfloat16)
    for device in range(COUNT):
        pack_ref[device] = pack


def weights(eta, folds, events, groups):
    return pl.pallas_call(
        weight_kernel,
        in_specs=[vmem()] * 4,
        out_specs=[vmem()] * 3,
        out_shape=[
            jax.ShapeDtypeStruct((HALF, ROWS), jnp.float32),
            jax.ShapeDtypeStruct((HALF, ROWS), jnp.float32),
            jax.ShapeDtypeStruct((COUNT, HALF, 2 * SLOTS), jnp.bfloat16),
        ],
        compiler_params=pltpu.CompilerParams(vmem_limit_bytes=16 * MIB),
        cost_estimate=pl.CostEstimate(flops=10**8, bytes_accessed=10**6, transcendentals=0),
    )(eta, folds, events, groups)


def resid_kernel(pack_ref, weight_ref, counted_ref, groups_ref, resid_ref):
    mine = lax.axis_index("subj")
    base = mine * (SLOTS - 1)
    wide = 2 * SLOTS
    source = lax.broadcasted_iota(jnp.int32, (wide, 3 * wide), 0)
    target = lax.broadcasted_iota(jnp.int32, (wide, 3 * wide), 1)
    suffix_part = (target < SLOTS) & (source >= target) & (source < SLOTS)
    total_part = (target >= wide) & (target < 2 * wide) & (source < SLOTS)
    count_part = (target >= 2 * wide) & (source - SLOTS == target - 2 * wide)
    matrix = jnp.where(suffix_part | total_part | count_part, 1.0, 0.0).astype(jnp.bfloat16)
    flat = pack_ref[...].astype(jnp.float32).reshape(COUNT * HALF, wide).astype(jnp.bfloat16)
    sums = jnp.dot(flat, matrix, preferred_element_type=jnp.float32)
    zero = jnp.zeros((HALF, wide), jnp.float32)
    after, before, own = zero, zero, zero
    for device in reversed(range(COUNT)):
        part = sums[device * HALF : device * HALF + HALF]
        count = part[:, 2 * wide :]
        some = count > 0
        risk = jnp.where(some, part[:, :wide] + after, 1.0)
        added = jnp.where(some, count / risk, 0.0)
        after = after + part[:, wide : 2 * wide]
        before = before + jnp.where(device < mine, added, 0.0)
        own = own + jnp.where(device == mine, added, 0.0)
    slot = lax.broadcasted_iota(jnp.int32, (wide, ROWS), 0)
    upto = (slot <= groups_ref[...] - base).astype(jnp.bfloat16)
    high, mid, low = parts3(own)
    hazard = jnp.dot(high, upto, preferred_element_type=jnp.float32) + (
        jnp.dot(mid, upto, preferred_element_type=jnp.float32)
        + jnp.dot(low, upto, preferred_element_type=jnp.float32)
    )
    hazard = hazard + jnp.sum(before, axis=1, keepdims=True)
    resid = counted_ref[...] - weight_ref[...] * hazard
    resid_ref[...] = resid.astype(jnp.bfloat16)


def residuals(pack, weight, counted, groups):
    return pl.pallas_call(
        resid_kernel,
        in_specs=[vmem()] * 4,
        out_specs=vmem(),
        out_shape=jax.ShapeDtypeStruct((HALF, ROWS), jnp.bfloat16),
        compiler_params=pltpu.CompilerParams(vmem_limit_bytes=16 * MIB),
        cost_estimate=pl.CostEstimate(flops=10**8, bytes_accessed=10**6, transcendentals=0),
    )(pack, weight, counted, groups)


def grad_kernel(geno_ref, own_ref, other_ref, out_ref):
    first = (lax.axis_index("var") & 1) == 0
    own = own_ref[...].astype(jnp.float32)
    other = other_ref[...].astype(jnp.float32)
    turned = jnp.concatenate(
        [jnp.where(first, own, other), jnp.where(first, other, own)], axis=0
    ).astype(jnp.bfloat16)
    wide = 2048
    for at in range(0, geno_ref.shape[1], wide):
        block = jnp.dot(turned, geno_ref[:, at : at + wide], preferred_element_type=jnp.float32)
        block = block * SCALE
        for piece in range(wide // 128):
            out_ref[at // 128 + piece] = block[:, 128 * piece : 128 * piece + 128]


def grad_slots(genotype, own, other):
    rows, depth = genotype.shape
    return pl.pallas_call(
        grad_kernel,
        in_specs=[vmem()] * 3,
        out_specs=vmem(),
        out_shape=jax.ShapeDtypeStruct((depth // 128, COLS, 128), jnp.float32),
        compiler_params=pltpu.CompilerParams(vmem_limit_bytes=32 * MIB),
        cost_estimate=pl.CostEstimate(
            flops=2 * rows * depth * 128, bytes_accessed=rows * depth * 2, transcendentals=0
        ),
    )(genotype, own, other)


def swap(value, masks):
    pairs = [(index, index ^ masks[index & 1]) for index in range(8)]
    return lax.ppermute(value, "var", pairs)


def per_device(genotype, coefs, events, folds, groups):
    events = events.reshape(1, ROWS)
    groups = groups.reshape(1, ROWS)

    eta, held = eta_halves(genotype, pltpu.with_memory_space_constraint(coefs.T, pltpu.HBM))
    eta = eta[0] + swap(eta[1], (1, 1))
    sent = eta.astype(jnp.float16)
    for masks in ((2, 6), (6, 2), (4, 4)):
        eta = eta + swap(sent, masks).astype(jnp.float32)
    weight, counted, pack = weights(eta, folds.T, events, groups)
    pack = lax.all_to_all(pack, "subj", 0, 0)
    own = residuals(pack, weight, counted, groups)
    other = swap(own, (1, 1))
    slots = grad_slots(held, own, other).astype(jnp.float16)
    slots = lax.all_to_all(slots, "subj", 0, 0)
    factor = -1.0 / (SCALE * float(COUNT * ROWS) ** 0.5)
    return (jnp.sum(slots.astype(jnp.float32), axis=0) * factor).T


def solution(mesh):
    in_specs = (P("subj", "var"), P("var", None), P("subj"), P("subj", None), P("subj"))
    out_specs = P(("var", "subj"), None)
    return jax.shard_map(
        per_device, mesh=mesh, in_specs=in_specs, out_specs=out_specs, check_vma=False
    )
```

time: 73 us -> 62.5 us (0.86)
  local copies, waits for them, and re-layouts: 4.3 us -> 0.02 us
  Pallas kernels: 13 us -> 9.34 us
  other arithmetic: 3.15 us -> 0.79 us
    pallas_call x4, Pallas kernels: 13 us -> 9.34 us  [the longest x1 6.56 us: eta_halves(): pl.pallas_call(eta_kernel, in_specs=[hbm(), hbm()], out_specs=[vmem(), vm...]
    unnamed x10 -> x6, local copies, waits for them, and re-layouts: 3.4 us -> 0.01 us
    convert_element_type x1, other arithmetic: 0.91 us -> 0.01 us  [per_device(): sent = eta.astype(jnp.float16)]
    squeeze x1, local copies, waits for them, and re-layouts: 0.9 us -> 0.01 us  [per_device(): eta = eta[0] + swap(eta[1], (1, 1))]
    add x1, other arithmetic: 0.92 us -> 0.03 us  [per_device(): eta = eta + swap(sent, masks).astype(jnp.float32)]
where the time goes in v3:
time: 62.5 us; the launch traced here: 62.4 us
  blocking collectives  41.1 us (66%)
  Pallas kernels  9.34 us (15%)
  waiting for transfers between devices  6.66 us (11%)
  starting transfers between devices  4.44 us (7%)
  other arithmetic  0.79 us (1%)
    all_to_all x1, blocking collectives, per_device(): pack = lax.all_to_all(pack, 'subj', 0, 0)  21.5 us
    all_to_all x1, blocking collectives, per_device(): slots = lax.all_to_all(slots, 'subj', 0, 0)  19.6 us
    ppermute x5, waiting for transfers between devices, swap(): return lax.ppermute(value, 'var', pairs)  6.66 us
    pallas_call x1, Pallas kernels, eta_halves(): pl.pallas_call(eta_kernel, in_specs=[hbm(), hbm()], out_specs=[vmem(), vm...  6.56 us
    ppermute x5, starting transfers between devices, swap(): return lax.ppermute(value, 'var', pairs)  4.44 us
    pallas_call x1, Pallas kernels, grad_slots(): pl.pallas_call(grad_kernel, in_specs=[vmem()] * 3, out_specs=vmem(), out_...  1.55 us
  transfers between devices with their start and end apart: 5, of which 4 were waited for; matrix products, arithmetic and copies ran while one was open for 0% of the time, Pallas kernels for 0%

profile of v3, /device:TPU:32, one launch (start us, length us, event | category | flops | bytes accessed | tf_op | source)
XLA Modules:
  0.0 62.4 jit_solution(11348021020604530307)
XLA Ops:
  0.0 0.0 copy-start
  0.0 0.0 copy-start.1
  0.0 0.0 copy-start.2
  0.0 6.6 %shard_map.55 = (f32[2,24,1024]{2,1,0:T(8,128)S(1)}, bf16[1024,4096]{1,0:T(8,128)(2,1)S(1)}) custom-call(bf16[1024,4096]{1,0:T(8,128)(2,1)} %geno_ref.1, bf16[48,4096]{1,0:T(8,128)(2,1)} %bitcast.18), custom_call_target="tpu_custom_call" | custom-call | flops 1073741824 | bytes 8388608 | tf_op jit(solution)/shard_map/pallas_call | solution.py:67
  6.6 0.1 collective-permute-start
  6.7 1.3 %collective-permute-done = f32[24,1024]{1,0:T(8,128)S(1)} collective-permute-done((f32[24,1024]{1,0:T(8,128)S(1)}, f32[24,1024]{1,0:T(8,128)S(1)}, u32[]{:S(2)}, u32[]{:S(2)}) %collective-permute-start) | collective-permute-done | bytes 98336 | tf_op jit(solution)/shard_map/ppermute | solution.py:202
  8.0 3.1 %collective-permute-start.3 = (f16[24,1024]{1,0:T(8,128)(2,1)S(1)}, f16[24,1024]{1,0:T(8,128)(2,1)S(1)}, u32[]{:S(2)}, u32[]{:S(2)}) collective-permute-start(f16[24,1024]{1,0:T(8,128)(2,1)S(1)} %fusion), channel_id=1, source_target_pairs={{0,4},{1,5},{2,6},{3,7},{4,0},{5,1},{6,2},{7,3},{8,12},{9,13},{10,... | collective-permute-start | bytes 147464 | tf_op jit(solution)/shard_map/ppermute | solution.py:202
  11.1 1.1 %collective-permute-start.2 = (f16[24,1024]{1,0:T(8,128)(2,1)S(1)}, f16[24,1024]{1,0:T(8,128)(2,1)S(1)}, u32[]{:S(2)}, u32[]{:S(2)}) collective-permute-start(f16[24,1024]{1,0:T(8,128)(2,1)S(1)} %fusion), channel_id=1, source_target_pairs={{0,6},{1,3},{2,4},{3,1},{4,2},{5,7},{6,0},{7,5},{8,14},{9,11},{10,... | collective-permute-start | bytes 147464 | tf_op jit(solution)/shard_map/ppermute | solution.py:202
  12.3 0.0 collective-permute-start.1
  12.3 1.4 %collective-permute-done.3 = f16[24,1024]{1,0:T(8,128)(2,1)S(1)} collective-permute-done((f16[24,1024]{1,0:T(8,128)(2,1)S(1)}, f16[24,1024]{1,0:T(8,128)(2,1)S(1)}, u32[]{:S(2)}, u32[]{:S(2)}) %collective-permute-start.3) | collective-permute-done | bytes 49184 | tf_op jit(solution)/shard_map/ppermute | solution.py:202
  13.7 2.7 %collective-permute-done.2 = f16[24,1024]{1,0:T(8,128)(2,1)S(1)} collective-permute-done((f16[24,1024]{1,0:T(8,128)(2,1)S(1)}, f16[24,1024]{1,0:T(8,128)(2,1)S(1)}, u32[]{:S(2)}, u32[]{:S(2)}) %collective-permute-start.2) | collective-permute-done | bytes 49184 | tf_op jit(solution)/shard_map/ppermute | solution.py:202
  16.4 0.0 collective-permute-done.1
  16.4 0.0 copy-done
  16.5 0.0 copy-done.1
  16.5 0.0 copy-done.2
  16.5 0.4 shard_map.56
  16.9 21.5 %all_to_all.10.pack_ref = bf16[32,24,128]{2,1,0:T(8,128)(2,1)S(1)} all-to-all(bf16[32,24,128]{2,1,0:T(8,128)(2,1)S(1)} %get-tuple-element.12), channel_id=1, replica_groups=mesh['subj'=32,'var'=8] {'subj'}, dimensions={0} | all-to-all | bytes 393216 | tf_op jit(solution)/shard_map/all_to_all | solution.py:215
  38.3 0.9 %shard_map.57.own_ref = bf16[24,1024]{1,0:T(8,128)(2,1)S(1)} custom-call(bf16[32,24,128]{2,1,0:T(8,128)(2,1)S(1)} %all_to_all.10.pack_ref, f32[24,1024]{1,0:T(8,128)S(1)} %get-tuple-element.13.weight_ref, f32[24,1024]{1,0:T(8,128)S(1)} %get-tuple-element.14.counted_ref, s32[1,1024]{1,0:T(1,128)S(1)} %bitcast.15), custom_call_target="tpu_custom_call" | custom-call | flops 100000000 | bytes 1000000 | tf_op jit(solution)/shard_map/pallas_call | solution.py:161
  39.2 0.1 collective-permute-start.4
  39.3 1.2 %collective-permute-done.4.other_ref = bf16[24,1024]{1,0:T(8,128)(2,1)S(1)} collective-permute-done((bf16[24,1024]{1,0:T(8,128)(2,1)S(1)}, bf16[24,1024]{1,0:T(8,128)(2,1)S(1)}, u32[]{:S(2)}, u32[]{:S(2)}) %collective-permute-start.4) | collective-permute-done | bytes 49184 | tf_op jit(solution)/shard_map/ppermute | solution.py:202
  40.5 1.5 %shard_map.58 = f32[32,48,128]{2,1,0:T(8,128)S(1)} custom-call(bf16[1024,4096]{1,0:T(8,128)(2,1)S(1)} %get-tuple-element.10.geno_ref, bf16[24,1024]{1,0:T(8,128)(2,1)S(1)} %shard_map.57.own_ref, bf16[24,1024]{1,0:T(8,128)(2,1)S(1)} %collective-permute-done.4.other_ref), custom_call_target="tpu_custom_call" | custom-call | flops 1073741824 | bytes 8388608 | tf_op jit(solution)/shard_map/pallas_call | solution.py:188
  42.1 0.1 convert_element_type.22
  42.1 19.6 %all_to_all.11 = f16[32,48,128]{2,1,0:T(8,128)(2,1)S(1)} all-to-all(f16[32,48,128]{2,1,0:T(8,128)(2,1)S(1)} %convert_element_type.22), channel_id=1, replica_groups=mesh['subj'=32,'var'=8] {'subj'}, dimensions={0} | all-to-all | bytes 786432 | tf_op jit(solution)/shard_map/all_to_all | solution.py:219
  61.7 0.1 convert_reduce_fusion
  61.8 0.6 multiply_bitcast_fusion
  (3 shorter events, 0.1 us)
Async XLA Ops:
  0.0 16.5 %copy-start = (s32[1024]{0:T(1024)S(1)}, s32[1024]{0:T(1024)}, u32[]{:S(2)}) copy-start(s32[1024]{0:T(1024)} %param.9) | copy-start | bytes 12292
  0.0 16.5 %copy-start.1 = (s32[1024,48]{0,1:T(8,128)S(1)}, s32[1024,48]{0,1:T(8,128)}, u32[]{:S(2)}) copy-start(s32[1024,48]{0,1:T(8,128)} %param.8) | copy-start | bytes 589828
  0.0 16.5 %copy-start.2 = (s32[1024]{0:T(1024)S(1)}, s32[1024]{0:T(1024)}, u32[]{:S(2)}) copy-start(s32[1024]{0:T(1024)} %param.7) | copy-start | bytes 12292
  6.6 1.4 %collective-permute-start = (f32[24,1024]{1,0:T(8,128)S(1)}, f32[24,1024]{1,0:T(8,128)S(1)}, u32[]{:S(2)}, u32[]{:S(2)}) collective-permute-start(f32[24,1024]{1,0:T(8,128)S(1)} %slice_bitcast_fusion), channel_id=1, source_target_pairs={{0,1},{1,0},{2,3},{3,2},{4,5},{5,4},{6,7},{7,6},{8,9},{9,8},{10,11... | collective-permute-start | bytes 294920 | tf_op jit(solution)/shard_map/ppermute | solution.py:202
  8.0 5.7 %collective-permute-start.3 = (f16[24,1024]{1,0:T(8,128)(2,1)S(1)}, f16[24,1024]{1,0:T(8,128)(2,1)S(1)}, u32[]{:S(2)}, u32[]{:S(2)}) collective-permute-start(f16[24,1024]{1,0:T(8,128)(2,1)S(1)} %fusion), channel_id=1, source_target_pairs={{0,4},{1,5},{2,6},{3,7},{4,0},{5,1},{6,2},{7,3},{8,12},{9,13},{10,... | collective-permute-start | bytes 147464 | tf_op jit(solution)/shard_map/ppermute | solution.py:202
  11.1 5.3 %collective-permute-start.2 = (f16[24,1024]{1,0:T(8,128)(2,1)S(1)}, f16[24,1024]{1,0:T(8,128)(2,1)S(1)}, u32[]{:S(2)}, u32[]{:S(2)}) collective-permute-start(f16[24,1024]{1,0:T(8,128)(2,1)S(1)} %fusion), channel_id=1, source_target_pairs={{0,6},{1,3},{2,4},{3,1},{4,2},{5,7},{6,0},{7,5},{8,14},{9,11},{10,... | collective-permute-start | bytes 147464 | tf_op jit(solution)/shard_map/ppermute | solution.py:202
  12.3 4.2 %collective-permute-start.1 = (f16[24,1024]{1,0:T(8,128)(2,1)S(1)}, f16[24,1024]{1,0:T(8,128)(2,1)S(1)}, u32[]{:S(2)}, u32[]{:S(2)}) collective-permute-start(f16[24,1024]{1,0:T(8,128)(2,1)S(1)} %fusion), channel_id=1, source_target_pairs={{0,2},{1,7},{2,0},{3,5},{4,6},{5,3},{6,4},{7,1},{8,10},{9,15},{10,... | collective-permute-start | bytes 147464 | tf_op jit(solution)/shard_map/ppermute | solution.py:202
  39.2 1.3 %collective-permute-start.4 = (bf16[24,1024]{1,0:T(8,128)(2,1)S(1)}, bf16[24,1024]{1,0:T(8,128)(2,1)S(1)}, u32[]{:S(2)}, u32[]{:S(2)}) collective-permute-start(bf16[24,1024]{1,0:T(8,128)(2,1)S(1)} %shard_map.57.own_ref), channel_id=1, source_target_pairs={{0,1},{1,0},{2,3},{3,2},{4,5},{5,4},{6,7},{7,6},{8,9},{9,8},{10,11... | collective-permute-start | bytes 147464 | tf_op jit(solution)/shard_map/ppermute | solution.py:202

commit v4 on v3

--- a/solution.py
+++ b/solution.py
@@ -30,36 +30,39 @@
     return pl.BlockSpec(memory_space=pltpu.HBM)
 
 
-def blocks(rows, depth):
-    return [(row, 512, at, 512) for row in range(0, rows, 512) for at in range(0, depth, 512)]
-
-
-def eta_kernel(geno_ref, coefs_ref, out_ref, held_ref, taken, sems, taken_sem):
+def blocks(depth):
+    widths = [256, 256] + [512] * (depth // 512 - 2) + [256, 256]
+    return [(sum(widths[:number]), wide) for number, wide in enumerate(widths)]
+
+
+def eta_kernel(geno_ref, coefs_ref, out_ref, held_ref, taken, geno_sems, coefs_sems):
     core = lax.axis_index("var") & 1
-    rows, depth = geno_ref.shape
-    pieces = blocks(rows, depth)
-    take = pltpu.make_async_copy(coefs_ref, taken, taken_sem)
-    take.start()
+    pieces = blocks(geno_ref.shape[1])
     copies = []
-    for number, (row, high, at, wide) in enumerate(pieces):
-        window = (pl.ds(row, high), pl.ds(at, wide))
-        copy = pltpu.make_async_copy(geno_ref.at[window], held_ref.at[window], sems.at[number])
-        copy.start()
-        copies.append(copy)
-    take.wait()
+    for number, (at, wide) in enumerate(pieces):
+        window = (slice(None), pl.ds(at, wide))
+        small = pltpu.make_async_copy(
+            coefs_ref.at[window], taken.at[window], coefs_sems.at[number]
+        )
+        large = pltpu.make_async_copy(
+            geno_ref.at[window], held_ref.at[window], geno_sems.at[number]
+        )
+        small.start()
+        large.start()
+        copies.append((small, large))
     total = None
-    for number, (row, high, at, wide) in enumerate(pieces):
-        copies[number].wait()
+    for (at, wide), (small, large) in zip(pieces, copies):
+        small.wait()
+        large.wait()
         block = lax.dot_general(
             taken[:, at : at + wide],
-            held_ref[row : row + high, at : at + wide],
+            held_ref[:, at : at + wide],
             (((1,), (1,)), ((), ())),
             preferred_element_type=jnp.float32,
         )
-        total = block if at == 0 else total + block
-        if at + wide == depth:
-            out_ref[core, :, row : row + high] = total[:HALF]
-            out_ref[1 - core, :, row : row + high] = total[HALF:]
+        total = block if total is None else total + block
+    out_ref[core] = total[:HALF]
+    out_ref[1 - core] = total[HALF:]
 
 
 def eta_halves(genotype, coefs):
@@ -74,8 +77,8 @@
         ],
         scratch_shapes=[
             pltpu.VMEM((COLS, depth), coefs.dtype),
-            pltpu.SemaphoreType.DMA((len(blocks(rows, depth)),)),
-            pltpu.SemaphoreType.DMA,
+            pltpu.SemaphoreType.DMA((len(blocks(depth)),)),
+            pltpu.SemaphoreType.DMA((len(blocks(depth)),)),
         ],
         compiler_params=pltpu.CompilerParams(vmem_limit_bytes=44 * MIB),
         cost_estimate=pl.CostEstimate(
@@ -197,8 +200,8 @@
     )(genotype, own, other)
 
 
-def swap(value, masks):
-    pairs = [(index, index ^ masks[index & 1]) for index in range(8)]
+def swap(value, mask):
+    pairs = [(index, index ^ mask) for index in range(8)]
     return lax.ppermute(value, "var", pairs)
 
 
@@ -207,14 +210,14 @@
     groups = groups.reshape(1, ROWS)
 
     eta, held = eta_halves(genotype, pltpu.with_memory_space_constraint(coefs.T, pltpu.HBM))
-    eta = eta[0] + swap(eta[1], (1, 1))
+    eta = eta[0] + swap(eta[1], 1)
     sent = eta.astype(jnp.float16)
-    for masks in ((2, 6), (6, 2), (4, 4)):
-        eta = eta + swap(sent, masks).astype(jnp.float32)
+    for mask in (2, 6, 4):
+        eta = eta + swap(sent, mask).astype(jnp.float32)
     weight, counted, pack = weights(eta, folds.T, events, groups)
     pack = lax.all_to_all(pack, "subj", 0, 0)
     own = residuals(pack, weight, counted, groups)
-    other = swap(own, (1, 1))
+    other = swap(own, 1)
     slots = grad_slots(held, own, other).astype(jnp.float16)
     slots = lax.all_to_all(slots, "subj", 0, 0)
     factor = -1.0 / (SCALE * float(COUNT * ROWS) ** 0.5)

time: 62.5 us -> 60.3 us (0.965)
  Pallas kernels: 9.34 us -> 7.05 us
    pallas_call x1, Pallas kernels: 6.56 us -> 4.27 us  [eta_halves(): pl.pallas_call(eta_kernel, in_specs=[hbm(), hbm()], out_specs=[vmem(), vm...]
where the time goes in v4:
time: 60.3 us; the launch traced here: 60.1 us
  blocking collectives  41.1 us (68%)
  Pallas kernels  7.05 us (12%)
  waiting for transfers between devices  6.66 us (11%)
  starting transfers between devices  4.44 us (7%)
  other arithmetic  0.79 us (1%)
    all_to_all x1, blocking collectives, per_device(): pack = lax.all_to_all(pack, 'subj', 0, 0)  21.6 us
    all_to_all x1, blocking collectives, per_device(): slots = lax.all_to_all(slots, 'subj', 0, 0)  19.5 us
    ppermute x5, waiting for transfers between devices, swap(): return lax.ppermute(value, 'var', pairs)  6.66 us
    ppermute x5, starting transfers between devices, swap(): return lax.ppermute(value, 'var', pairs)  4.44 us
    pallas_call x1, Pallas kernels, eta_halves(): pl.pallas_call(eta_kernel, in_specs=[hbm(), hbm()], out_specs=[vmem(), vm...  4.27 us
    pallas_call x1, Pallas kernels, grad_slots(): pl.pallas_call(grad_kernel, in_specs=[vmem()] * 3, out_specs=vmem(), out_...  1.54 us
  transfers between devices with their start and end apart: 5, of which 4 were waited for; matrix products, arithmetic and copies ran while one was open for 0% of the time, Pallas kernels for 0%

profile of v4, /device:TPU:32, one launch (start us, length us, event | category | flops | bytes accessed | tf_op | source)
XLA Modules:
  0.0 60.1 jit_solution(13879901223517084587)
XLA Ops:
  0.0 0.0 copy-start
  0.0 0.0 copy-start.1
  0.0 0.0 copy-start.2
  0.0 4.3 %shard_map.55 = (f32[2,24,1024]{2,1,0:T(8,128)S(1)}, bf16[1024,4096]{1,0:T(8,128)(2,1)S(1)}) custom-call(bf16[1024,4096]{1,0:T(8,128)(2,1)} %geno_ref.1, bf16[48,4096]{1,0:T(8,128)(2,1)} %bitcast.18), custom_call_target="tpu_custom_call" | custom-call | flops 1073741824 | bytes 8388608 | tf_op jit(solution)/shard_map/pallas_call | solution.py:70
  4.3 0.1 collective-permute-start
  4.4 1.3 %collective-permute-done = f32[24,1024]{1,0:T(8,128)S(1)} collective-permute-done((f32[24,1024]{1,0:T(8,128)S(1)}, f32[24,1024]{1,0:T(8,128)S(1)}, u32[]{:S(2)}, u32[]{:S(2)}) %collective-permute-start) | collective-permute-done | bytes 98336 | tf_op jit(solution)/shard_map/ppermute | solution.py:205
  5.7 3.1 %collective-permute-start.3 = (f16[24,1024]{1,0:T(8,128)(2,1)S(1)}, f16[24,1024]{1,0:T(8,128)(2,1)S(1)}, u32[]{:S(2)}, u32[]{:S(2)}) collective-permute-start(f16[24,1024]{1,0:T(8,128)(2,1)S(1)} %fusion), channel_id=1, source_target_pairs={{0,4},{1,5},{2,6},{3,7},{4,0},{5,1},{6,2},{7,3},{8,12},{9,13},{10,... | collective-permute-start | bytes 147464 | tf_op jit(solution)/shard_map/ppermute | solution.py:205
  8.8 1.1 %collective-permute-start.2 = (f16[24,1024]{1,0:T(8,128)(2,1)S(1)}, f16[24,1024]{1,0:T(8,128)(2,1)S(1)}, u32[]{:S(2)}, u32[]{:S(2)}) collective-permute-start(f16[24,1024]{1,0:T(8,128)(2,1)S(1)} %fusion), channel_id=1, source_target_pairs={{0,6},{1,7},{2,4},{3,5},{4,2},{5,3},{6,0},{7,1},{8,14},{9,15},{10,... | collective-permute-start | bytes 147464 | tf_op jit(solution)/shard_map/ppermute | solution.py:205
  10.0 0.0 collective-permute-start.1
  10.0 1.4 %collective-permute-done.3 = f16[24,1024]{1,0:T(8,128)(2,1)S(1)} collective-permute-done((f16[24,1024]{1,0:T(8,128)(2,1)S(1)}, f16[24,1024]{1,0:T(8,128)(2,1)S(1)}, u32[]{:S(2)}, u32[]{:S(2)}) %collective-permute-start.3) | collective-permute-done | bytes 49184 | tf_op jit(solution)/shard_map/ppermute | solution.py:205
  11.4 2.7 %collective-permute-done.2 = f16[24,1024]{1,0:T(8,128)(2,1)S(1)} collective-permute-done((f16[24,1024]{1,0:T(8,128)(2,1)S(1)}, f16[24,1024]{1,0:T(8,128)(2,1)S(1)}, u32[]{:S(2)}, u32[]{:S(2)}) %collective-permute-start.2) | collective-permute-done | bytes 49184 | tf_op jit(solution)/shard_map/ppermute | solution.py:205
  14.1 0.0 collective-permute-done.1
  14.2 0.0 copy-done
  14.2 0.0 copy-done.1
  14.2 0.0 copy-done.2
  14.2 0.4 shard_map.56
  14.6 21.6 %all_to_all.10.pack_ref = bf16[32,24,128]{2,1,0:T(8,128)(2,1)S(1)} all-to-all(bf16[32,24,128]{2,1,0:T(8,128)(2,1)S(1)} %get-tuple-element.12), channel_id=1, replica_groups=mesh['subj'=32,'var'=8] {'subj'}, dimensions={0} | all-to-all | bytes 393216 | tf_op jit(solution)/shard_map/all_to_all | solution.py:218
  36.1 0.8 %shard_map.57.own_ref = bf16[24,1024]{1,0:T(8,128)(2,1)S(1)} custom-call(bf16[32,24,128]{2,1,0:T(8,128)(2,1)S(1)} %all_to_all.10.pack_ref, f32[24,1024]{1,0:T(8,128)S(1)} %get-tuple-element.13.weight_ref, f32[24,1024]{1,0:T(8,128)S(1)} %get-tuple-element.14.counted_ref, s32[1,1024]{1,0:T(1,128)S(1)} %bitcast.15), custom_call_target="tpu_custom_call" | custom-call | flops 100000000 | bytes 1000000 | tf_op jit(solution)/shard_map/pallas_call | solution.py:164
  37.0 0.1 collective-permute-start.4
  37.1 1.2 %collective-permute-done.4.other_ref = bf16[24,1024]{1,0:T(8,128)(2,1)S(1)} collective-permute-done((bf16[24,1024]{1,0:T(8,128)(2,1)S(1)}, bf16[24,1024]{1,0:T(8,128)(2,1)S(1)}, u32[]{:S(2)}, u32[]{:S(2)}) %collective-permute-start.4) | collective-permute-done | bytes 49184 | tf_op jit(solution)/shard_map/ppermute | solution.py:205
  38.3 1.5 %shard_map.58 = f32[32,48,128]{2,1,0:T(8,128)S(1)} custom-call(bf16[1024,4096]{1,0:T(8,128)(2,1)S(1)} %get-tuple-element.10.geno_ref, bf16[24,1024]{1,0:T(8,128)(2,1)S(1)} %shard_map.57.own_ref, bf16[24,1024]{1,0:T(8,128)(2,1)S(1)} %collective-permute-done.4.other_ref), custom_call_target="tpu_custom_call" | custom-call | flops 1073741824 | bytes 8388608 | tf_op jit(solution)/shard_map/pallas_call | solution.py:191
  39.9 0.1 convert_element_type.22
  39.9 19.5 %all_to_all.11 = f16[32,48,128]{2,1,0:T(8,128)(2,1)S(1)} all-to-all(f16[32,48,128]{2,1,0:T(8,128)(2,1)S(1)} %convert_element_type.22), channel_id=1, replica_groups=mesh['subj'=32,'var'=8] {'subj'}, dimensions={0} | all-to-all | bytes 786432 | tf_op jit(solution)/shard_map/all_to_all | solution.py:222
  59.4 0.1 convert_reduce_fusion
  59.5 0.6 %multiply_bitcast_fusion = f32[128,48]{0,1:T(8,128)} fusion(f32[48,128]{1,0:T(8,128)S(1)} %convert_reduce_fusion), kind=kLoop, calls=%fused_computation.5 | loop fusion | flops 6144 | bytes 49152 | tf_op jit(solution)/shard_map/mul | solution.py:224
  (3 shorter events, 0.1 us)
Async XLA Ops:
  0.0 14.2 %copy-start = (s32[1024]{0:T(1024)S(1)}, s32[1024]{0:T(1024)}, u32[]{:S(2)}) copy-start(s32[1024]{0:T(1024)} %param.9) | copy-start | bytes 12292
  0.0 14.2 %copy-start.1 = (s32[1024,48]{0,1:T(8,128)S(1)}, s32[1024,48]{0,1:T(8,128)}, u32[]{:S(2)}) copy-start(s32[1024,48]{0,1:T(8,128)} %param.8) | copy-start | bytes 589828
  0.0 14.2 %copy-start.2 = (s32[1024]{0:T(1024)S(1)}, s32[1024]{0:T(1024)}, u32[]{:S(2)}) copy-start(s32[1024]{0:T(1024)} %param.7) | copy-start | bytes 12292
  4.3 1.4 %collective-permute-start = (f32[24,1024]{1,0:T(8,128)S(1)}, f32[24,1024]{1,0:T(8,128)S(1)}, u32[]{:S(2)}, u32[]{:S(2)}) collective-permute-start(f32[24,1024]{1,0:T(8,128)S(1)} %slice_bitcast_fusion), channel_id=1, source_target_pairs={{0,1},{1,0},{2,3},{3,2},{4,5},{5,4},{6,7},{7,6},{8,9},{9,8},{10,11... | collective-permute-start | bytes 294920 | tf_op jit(solution)/shard_map/ppermute | solution.py:205
  5.7 5.7 %collective-permute-start.3 = (f16[24,1024]{1,0:T(8,128)(2,1)S(1)}, f16[24,1024]{1,0:T(8,128)(2,1)S(1)}, u32[]{:S(2)}, u32[]{:S(2)}) collective-permute-start(f16[24,1024]{1,0:T(8,128)(2,1)S(1)} %fusion), channel_id=1, source_target_pairs={{0,4},{1,5},{2,6},{3,7},{4,0},{5,1},{6,2},{7,3},{8,12},{9,13},{10,... | collective-permute-start | bytes 147464 | tf_op jit(solution)/shard_map/ppermute | solution.py:205
  8.8 5.3 %collective-permute-start.2 = (f16[24,1024]{1,0:T(8,128)(2,1)S(1)}, f16[24,1024]{1,0:T(8,128)(2,1)S(1)}, u32[]{:S(2)}, u32[]{:S(2)}) collective-permute-start(f16[24,1024]{1,0:T(8,128)(2,1)S(1)} %fusion), channel_id=1, source_target_pairs={{0,6},{1,7},{2,4},{3,5},{4,2},{5,3},{6,0},{7,1},{8,14},{9,15},{10,... | collective-permute-start | bytes 147464 | tf_op jit(solution)/shard_map/ppermute | solution.py:205
  10.0 4.2 %collective-permute-start.1 = (f16[24,1024]{1,0:T(8,128)(2,1)S(1)}, f16[24,1024]{1,0:T(8,128)(2,1)S(1)}, u32[]{:S(2)}, u32[]{:S(2)}) collective-permute-start(f16[24,1024]{1,0:T(8,128)(2,1)S(1)} %fusion), channel_id=1, source_target_pairs={{0,2},{1,3},{2,0},{3,1},{4,6},{5,7},{6,4},{7,5},{8,10},{9,11},{10,... | collective-permute-start | bytes 147464 | tf_op jit(solution)/shard_map/ppermute | solution.py:205
  37.0 1.3 %collective-permute-start.4 = (bf16[24,1024]{1,0:T(8,128)(2,1)S(1)}, bf16[24,1024]{1,0:T(8,128)(2,1)S(1)}, u32[]{:S(2)}, u32[]{:S(2)}) collective-permute-start(bf16[24,1024]{1,0:T(8,128)(2,1)S(1)} %shard_map.57.own_ref), channel_id=1, source_target_pairs={{0,1},{1,0},{2,3},{3,2},{4,5},{5,4},{6,7},{7,6},{8,9},{9,8},{10,11... | collective-permute-start | bytes 147464 | tf_op jit(solution)/shard_map/ppermute | solution.py:205

commit v5 on v4

--- a/solution.py
+++ b/solution.py
@@ -14,12 +14,9 @@
 SCALE = 0.125
 
 
-def parts3(value):
+def parts(value):
     high = value.astype(jnp.bfloat16)
-    rest = value - high.astype(jnp.float32)
-    mid = rest.astype(jnp.bfloat16)
-    low = (rest - mid.astype(jnp.float32)).astype(jnp.bfloat16)
-    return high, mid, low
+    return high, (value - high.astype(jnp.float32)).astype(jnp.bfloat16)
 
 
 def vmem():
@@ -87,88 +84,111 @@
     )(genotype, coefs)
 
 
-def weight_kernel(eta_ref, folds_ref, events_ref, groups_ref, weight_ref, counted_ref, pack_ref):
+def rows_dot(left, right):
+    return lax.dot_general(
+        left, right, (((1,), (1,)), ((), ())), preferred_element_type=jnp.float32
+    )
+
+
+def plan_kernel(folds_ref, events_ref, groups_ref, fold_ref, counted_ref, hot_ref, upto_ref, count_ref, scan_ref):
     core = lax.axis_index("var") & 1
     base = lax.axis_index("subj") * (SLOTS - 1)
     fold = folds_ref[pl.ds(pl.multiple_of(core * HALF, 8), HALF), :].astype(jnp.float32)
-    weight = fold * jnp.exp(eta_ref[...])
     counted = fold * events_ref[...].astype(jnp.float32)
-    weight_ref[...] = weight
+    fold_ref[...] = fold
     counted_ref[...] = counted
     slot = lax.broadcasted_iota(jnp.int32, (SLOTS, ROWS), 0)
-    hot = (slot == groups_ref[...] - base).astype(jnp.bfloat16)
-
-    def total(part):
-        return lax.dot_general(
-            part, hot, (((1,), (1,)), ((), ())), preferred_element_type=jnp.float32
-        )
-
-    high, mid, low = parts3(weight)
-    sums = total(high) + (total(mid) + total(low))
-    pack = jnp.concatenate([sums, total(counted.astype(jnp.bfloat16))], axis=1).astype(jnp.bfloat16)
-    for device in range(COUNT):
-        pack_ref[device] = pack
-
-
-def weights(eta, folds, events, groups):
-    return pl.pallas_call(
-        weight_kernel,
-        in_specs=[vmem()] * 4,
-        out_specs=[vmem()] * 3,
+    group = groups_ref[...] - base
+    hot = (slot == group).astype(jnp.bfloat16)
+    hot_ref[...] = hot
+    upto_ref[...] = (slot <= group).astype(jnp.bfloat16)
+    count_ref[...] = rows_dot(counted.astype(jnp.bfloat16), hot)
+    wide = 2 * SLOTS
+    source = lax.broadcasted_iota(jnp.int32, (wide, 2 * wide), 0)
+    target = lax.broadcasted_iota(jnp.int32, (wide, 2 * wide), 1)
+    suffix_part = (target < SLOTS) & (source >= target) & (source < SLOTS)
+    total_part = (target >= wide) & (source < SLOTS)
+    scan_ref[...] = jnp.where(suffix_part | total_part, 1.0, 0.0).astype(jnp.bfloat16)
+
+
+def plan(folds, events, groups):
+    return pl.pallas_call(
+        plan_kernel,
+        in_specs=[vmem()] * 3,
+        out_specs=[vmem()] * 6,
         out_shape=[
             jax.ShapeDtypeStruct((HALF, ROWS), jnp.float32),
             jax.ShapeDtypeStruct((HALF, ROWS), jnp.float32),
-            jax.ShapeDtypeStruct((COUNT, HALF, 2 * SLOTS), jnp.bfloat16),
+            jax.ShapeDtypeStruct((SLOTS, ROWS), jnp.bfloat16),
+            jax.ShapeDtypeStruct((SLOTS, ROWS), jnp.bfloat16),
+            jax.ShapeDtypeStruct((HALF, SLOTS), jnp.float32),
+            jax.ShapeDtypeStruct((2 * SLOTS, 4 * SLOTS), jnp.bfloat16),
         ],
         compiler_params=pltpu.CompilerParams(vmem_limit_bytes=16 * MIB),
         cost_estimate=pl.CostEstimate(flops=10**8, bytes_accessed=10**6, transcendentals=0),
-    )(eta, folds, events, groups)
-
-
-def resid_kernel(pack_ref, weight_ref, counted_ref, groups_ref, resid_ref):
+    )(folds, events, groups)
+
+
+def weight_kernel(eta_ref, fold_ref, hot_ref, count_ref, weight_ref, pack_ref):
+    weight = fold_ref[...] * jnp.exp(eta_ref[...])
+    weight_ref[...] = weight
+    high, low = parts(weight)
+    sums = rows_dot(high, hot_ref[...]) + rows_dot(low, hot_ref[...])
+    pack = jnp.concatenate([sums, count_ref[...]], axis=1).astype(jnp.bfloat16)
+    for device in range(COUNT):
+        pack_ref[device] = pack
+
+
+def weights(eta, fold, hot, count):
+    return pl.pallas_call(
+        weight_kernel,
+        in_specs=[vmem()] * 4,
+        out_specs=[vmem()] * 2,
+        out_shape=[
+            jax.ShapeDtypeStruct((HALF, ROWS), jnp.float32),
+            jax.ShapeDtypeStruct((COUNT, HALF, 2 * SLOTS), jnp.bfloat16),
+        ],
+        compiler_params=pltpu.CompilerParams(vmem_limit_bytes=16 * MIB),
+        cost_estimate=pl.CostEstimate(flops=10**8, bytes_accessed=10**6, transcendentals=0),
+    )(eta, fold, hot, count)
+
+
+def resid_kernel(pack_ref, weight_ref, counted_ref, upto_ref, scan_ref, resid_ref):
     mine = lax.axis_index("subj")
-    base = mine * (SLOTS - 1)
     wide = 2 * SLOTS
-    source = lax.broadcasted_iota(jnp.int32, (wide, 3 * wide), 0)
-    target = lax.broadcasted_iota(jnp.int32, (wide, 3 * wide), 1)
-    suffix_part = (target < SLOTS) & (source >= target) & (source < SLOTS)
-    total_part = (target >= wide) & (target < 2 * wide) & (source < SLOTS)
-    count_part = (target >= 2 * wide) & (source - SLOTS == target - 2 * wide)
-    matrix = jnp.where(suffix_part | total_part | count_part, 1.0, 0.0).astype(jnp.bfloat16)
-    flat = pack_ref[...].astype(jnp.float32).reshape(COUNT * HALF, wide).astype(jnp.bfloat16)
-    sums = jnp.dot(flat, matrix, preferred_element_type=jnp.float32)
+    flat = pack_ref[...].astype(jnp.float32).reshape(COUNT * HALF, wide)
+    sums = jnp.dot(flat.astype(jnp.bfloat16), scan_ref[...], preferred_element_type=jnp.float32)
+    counts = pltpu.roll(flat, SLOTS, 1)
     zero = jnp.zeros((HALF, wide), jnp.float32)
     after, before, own = zero, zero, zero
     for device in reversed(range(COUNT)):
         part = sums[device * HALF : device * HALF + HALF]
-        count = part[:, 2 * wide :]
+        count = counts[device * HALF : device * HALF + HALF]
         some = count > 0
         risk = jnp.where(some, part[:, :wide] + after, 1.0)
         added = jnp.where(some, count / risk, 0.0)
-        after = after + part[:, wide : 2 * wide]
+        after = after + part[:, wide:]
         before = before + jnp.where(device < mine, added, 0.0)
         own = own + jnp.where(device == mine, added, 0.0)
-    slot = lax.broadcasted_iota(jnp.int32, (wide, ROWS), 0)
-    upto = (slot <= groups_ref[...] - base).astype(jnp.bfloat16)
-    high, mid, low = parts3(own)
-    hazard = jnp.dot(high, upto, preferred_element_type=jnp.float32) + (
-        jnp.dot(mid, upto, preferred_element_type=jnp.float32)
-        + jnp.dot(low, upto, preferred_element_type=jnp.float32)
+    before = jnp.where(lax.broadcasted_iota(jnp.int32, (HALF, wide), 1) < SLOTS, before, 0.0)
+    high, low = parts(own[:, :SLOTS])
+    hazard = jnp.dot(high, upto_ref[...], preferred_element_type=jnp.float32) + jnp.dot(
+        low, upto_ref[...], preferred_element_type=jnp.float32
     )
     hazard = hazard + jnp.sum(before, axis=1, keepdims=True)
     resid = counted_ref[...] - weight_ref[...] * hazard
     resid_ref[...] = resid.astype(jnp.bfloat16)
 
 
-def residuals(pack, weight, counted, groups):
+def residuals(pack, weight, counted, upto, scan):
     return pl.pallas_call(
         resid_kernel,
-        in_specs=[vmem()] * 4,
+        in_specs=[vmem()] * 5,
         out_specs=vmem(),
         out_shape=jax.ShapeDtypeStruct((HALF, ROWS), jnp.bfloat16),
         compiler_params=pltpu.CompilerParams(vmem_limit_bytes=16 * MIB),
         cost_estimate=pl.CostEstimate(flops=10**8, bytes_accessed=10**6, transcendentals=0),
-    )(pack, weight, counted, groups)
+    )(pack, weight, counted, upto, scan)
 
 
 def grad_kernel(geno_ref, own_ref, other_ref, out_ref):
@@ -210,13 +230,14 @@
     groups = groups.reshape(1, ROWS)
 
     eta, held = eta_halves(genotype, pltpu.with_memory_space_constraint(coefs.T, pltpu.HBM))
+    fold, counted, hot, upto, count, scan = plan(folds.T, events, groups)
     eta = eta[0] + swap(eta[1], 1)
     sent = eta.astype(jnp.float16)
     for mask in (2, 6, 4):
         eta = eta + swap(sent, mask).astype(jnp.float32)
-    weight, counted, pack = weights(eta, folds.T, events, groups)
+    weight, pack = weights(eta, fold, hot, count)
     pack = lax.all_to_all(pack, "subj", 0, 0)
-    own = residuals(pack, weight, counted, groups)
+    own = residuals(pack, weight, counted, upto, scan)
     other = swap(own, 1)
     slots = grad_slots(held, own, other).astype(jnp.float16)
     slots = lax.all_to_all(slots, "subj", 0, 0)

time: 60.3 us -> 59.8 us (level)
  no operation moved by 1% of the time
where the time goes in v5:
time: 59.8 us; the launch traced here: 59.7 us
  blocking collectives  41.1 us (69%)
  Pallas kernels  6.82 us (11%)
  waiting for transfers between devices  6.47 us (11%)
  starting transfers between devices  4.44 us (7%)
  other arithmetic  0.78 us (1%)
    all_to_all x1, blocking collectives, per_device(): pack = lax.all_to_all(pack, 'subj', 0, 0)  21.6 us
    all_to_all x1, blocking collectives, per_device(): slots = lax.all_to_all(slots, 'subj', 0, 0)  19.5 us
    ppermute x5, waiting for transfers between devices, swap(): return lax.ppermute(value, 'var', pairs)  6.47 us
    ppermute x5, starting transfers between devices, swap(): return lax.ppermute(value, 'var', pairs)  4.44 us
    pallas_call x1, Pallas kernels, eta_halves(): pl.pallas_call(eta_kernel, in_specs=[hbm(), hbm()], out_specs=[vmem(), vm...  4.27 us
    pallas_call x1, Pallas kernels, grad_slots(): pl.pallas_call(grad_kernel, in_specs=[vmem()] * 3, out_specs=vmem(), out_...  1.55 us
  transfers between devices with their start and end apart: 5, of which 4 were waited for; matrix products, arithmetic and copies ran while one was open for 0% of the time, Pallas kernels for 0%

profile of v5, /device:TPU:32, one launch (start us, length us, event | category | flops | bytes accessed | tf_op | source)
XLA Modules:
  0.0 59.7 jit_solution(13883415233713222158)
XLA Ops:
  0.0 0.0 copy-start
  0.0 0.0 copy-start.1
  0.0 0.0 copy-start.2
  0.0 4.3 %shard_map.55 = (f32[2,24,1024]{2,1,0:T(8,128)S(1)}, bf16[1024,4096]{1,0:T(8,128)(2,1)S(1)}) custom-call(bf16[1024,4096]{1,0:T(8,128)(2,1)} %geno_ref.1, bf16[48,4096]{1,0:T(8,128)(2,1)} %bitcast.17), custom_call_target="tpu_custom_call" | custom-call | flops 1073741824 | bytes 8388608 | tf_op jit(solution)/shard_map/pallas_call | solution.py:67
  4.3 0.1 collective-permute-start
  4.4 1.3 %collective-permute-done = f32[24,1024]{1,0:T(8,128)S(1)} collective-permute-done((f32[24,1024]{1,0:T(8,128)S(1)}, f32[24,1024]{1,0:T(8,128)S(1)}, u32[]{:S(2)}, u32[]{:S(2)}) %collective-permute-start) | collective-permute-done | bytes 98336 | tf_op jit(solution)/shard_map/ppermute | solution.py:225
  5.7 3.1 %collective-permute-start.3 = (f16[24,1024]{1,0:T(8,128)(2,1)S(1)}, f16[24,1024]{1,0:T(8,128)(2,1)S(1)}, u32[]{:S(2)}, u32[]{:S(2)}) collective-permute-start(f16[24,1024]{1,0:T(8,128)(2,1)S(1)} %fusion), channel_id=1, source_target_pairs={{0,4},{1,5},{2,6},{3,7},{4,0},{5,1},{6,2},{7,3},{8,12},{9,13},{10,... | collective-permute-start | bytes 147464 | tf_op jit(solution)/shard_map/ppermute | solution.py:225
  8.8 1.1 %collective-permute-start.2 = (f16[24,1024]{1,0:T(8,128)(2,1)S(1)}, f16[24,1024]{1,0:T(8,128)(2,1)S(1)}, u32[]{:S(2)}, u32[]{:S(2)}) collective-permute-start(f16[24,1024]{1,0:T(8,128)(2,1)S(1)} %fusion), channel_id=1, source_target_pairs={{0,6},{1,7},{2,4},{3,5},{4,2},{5,3},{6,0},{7,1},{8,14},{9,15},{10,... | collective-permute-start | bytes 147464 | tf_op jit(solution)/shard_map/ppermute | solution.py:225
  10.0 0.0 collective-permute-start.1
  10.0 0.0 copy-done
  10.0 0.0 copy-done.1
  10.0 0.0 copy-done.2
  10.0 0.2 shard_map.56
  10.2 1.2 %collective-permute-done.3 = f16[24,1024]{1,0:T(8,128)(2,1)S(1)} collective-permute-done((f16[24,1024]{1,0:T(8,128)(2,1)S(1)}, f16[24,1024]{1,0:T(8,128)(2,1)S(1)}, u32[]{:S(2)}, u32[]{:S(2)}) %collective-permute-start.3) | collective-permute-done | bytes 49184 | tf_op jit(solution)/shard_map/ppermute | solution.py:225
  11.4 2.7 %collective-permute-done.2 = f16[24,1024]{1,0:T(8,128)(2,1)S(1)} collective-permute-done((f16[24,1024]{1,0:T(8,128)(2,1)S(1)}, f16[24,1024]{1,0:T(8,128)(2,1)S(1)}, u32[]{:S(2)}, u32[]{:S(2)}) %collective-permute-start.2) | collective-permute-done | bytes 49184 | tf_op jit(solution)/shard_map/ppermute | solution.py:225
  14.1 0.0 collective-permute-done.1
  14.2 0.2 shard_map.57
  14.4 21.6 %all_to_all.10.pack_ref = bf16[32,24,128]{2,1,0:T(8,128)(2,1)S(1)} all-to-all(bf16[32,24,128]{2,1,0:T(8,128)(2,1)S(1)} %get-tuple-element.20), channel_id=1, replica_groups=mesh['subj'=32,'var'=8] {'subj'}, dimensions={0} | all-to-all | bytes 393216 | tf_op jit(solution)/shard_map/all_to_all | solution.py:239
  35.9 0.6 %shard_map.58.own_ref = bf16[24,1024]{1,0:T(8,128)(2,1)S(1)} custom-call(bf16[32,24,128]{2,1,0:T(8,128)(2,1)S(1)} %all_to_all.10.pack_ref, f32[24,1024]{1,0:T(8,128)S(1)} %get-tuple-element.21.weight_ref, f32[24,1024]{1,0:T(8,128)S(1)} %get-tuple-element.22.counted_ref, bf16[64,1024]{1,0:T(8,128)(2,1)S(1)} %get-tuple-element.23.upto_ref, ...), custom_call_target="tpu_custom_call" | custom-call | flops 100000000 | bytes 1000000 | tf_op jit(solution)/shard_map/pallas_call | solution.py:184
  36.6 0.1 collective-permute-start.4
  36.7 1.2 %collective-permute-done.4.other_ref = bf16[24,1024]{1,0:T(8,128)(2,1)S(1)} collective-permute-done((bf16[24,1024]{1,0:T(8,128)(2,1)S(1)}, bf16[24,1024]{1,0:T(8,128)(2,1)S(1)}, u32[]{:S(2)}, u32[]{:S(2)}) %collective-permute-start.4) | collective-permute-done | bytes 49184 | tf_op jit(solution)/shard_map/ppermute | solution.py:225
  37.9 1.5 %shard_map.59 = f32[32,48,128]{2,1,0:T(8,128)S(1)} custom-call(bf16[1024,4096]{1,0:T(8,128)(2,1)S(1)} %get-tuple-element.15.geno_ref, bf16[24,1024]{1,0:T(8,128)(2,1)S(1)} %shard_map.58.own_ref, bf16[24,1024]{1,0:T(8,128)(2,1)S(1)} %collective-permute-done.4.other_ref), custom_call_target="tpu_custom_call" | custom-call | flops 1073741824 | bytes 8388608 | tf_op jit(solution)/shard_map/pallas_call | solution.py:211
  39.4 0.1 convert_element_type.22
  39.5 19.5 %all_to_all.11 = f16[32,48,128]{2,1,0:T(8,128)(2,1)S(1)} all-to-all(f16[32,48,128]{2,1,0:T(8,128)(2,1)S(1)} %convert_element_type.22), channel_id=1, replica_groups=mesh['subj'=32,'var'=8] {'subj'}, dimensions={0} | all-to-all | bytes 786432 | tf_op jit(solution)/shard_map/all_to_all | solution.py:243
  59.0 0.1 convert_reduce_fusion
  59.1 0.6 %multiply_bitcast_fusion = f32[128,48]{0,1:T(8,128)} fusion(f32[48,128]{1,0:T(8,128)S(1)} %convert_reduce_fusion), kind=kLoop, calls=%fused_computation.5 | loop fusion | flops 6144 | bytes 49152 | tf_op jit(solution)/shard_map/mul | solution.py:245
  (3 shorter events, 0.1 us)
Async XLA Ops:
  0.0 10.0 %copy-start = (s32[1024,48]{0,1:T(8,128)S(1)}, s32[1024,48]{0,1:T(8,128)}, u32[]{:S(2)}) copy-start(s32[1024,48]{0,1:T(8,128)} %param.8) | copy-start | bytes 589828
  0.0 10.0 %copy-start.1 = (s32[1024]{0:T(1024)S(1)}, s32[1024]{0:T(1024)}, u32[]{:S(2)}) copy-start(s32[1024]{0:T(1024)} %param.7) | copy-start | bytes 12292
  0.0 10.0 %copy-start.2 = (s32[1024]{0:T(1024)S(1)}, s32[1024]{0:T(1024)}, u32[]{:S(2)}) copy-start(s32[1024]{0:T(1024)} %param.9) | copy-start | bytes 12292
  4.3 1.4 %collective-permute-start = (f32[24,1024]{1,0:T(8,128)S(1)}, f32[24,1024]{1,0:T(8,128)S(1)}, u32[]{:S(2)}, u32[]{:S(2)}) collective-permute-start(f32[24,1024]{1,0:T(8,128)S(1)} %slice_bitcast_fusion), channel_id=1, source_target_pairs={{0,1},{1,0},{2,3},{3,2},{4,5},{5,4},{6,7},{7,6},{8,9},{9,8},{10,11... | collective-permute-start | bytes 294920 | tf_op jit(solution)/shard_map/ppermute | solution.py:225
  5.7 5.7 %collective-permute-start.3 = (f16[24,1024]{1,0:T(8,128)(2,1)S(1)}, f16[24,1024]{1,0:T(8,128)(2,1)S(1)}, u32[]{:S(2)}, u32[]{:S(2)}) collective-permute-start(f16[24,1024]{1,0:T(8,128)(2,1)S(1)} %fusion), channel_id=1, source_target_pairs={{0,4},{1,5},{2,6},{3,7},{4,0},{5,1},{6,2},{7,3},{8,12},{9,13},{10,... | collective-permute-start | bytes 147464 | tf_op jit(solution)/shard_map/ppermute | solution.py:225
  8.8 5.3 %collective-permute-start.2 = (f16[24,1024]{1,0:T(8,128)(2,1)S(1)}, f16[24,1024]{1,0:T(8,128)(2,1)S(1)}, u32[]{:S(2)}, u32[]{:S(2)}) collective-permute-start(f16[24,1024]{1,0:T(8,128)(2,1)S(1)} %fusion), channel_id=1, source_target_pairs={{0,6},{1,7},{2,4},{3,5},{4,2},{5,3},{6,0},{7,1},{8,14},{9,15},{10,... | collective-permute-start | bytes 147464 | tf_op jit(solution)/shard_map/ppermute | solution.py:225
  10.0 4.2 %collective-permute-start.1 = (f16[24,1024]{1,0:T(8,128)(2,1)S(1)}, f16[24,1024]{1,0:T(8,128)(2,1)S(1)}, u32[]{:S(2)}, u32[]{:S(2)}) collective-permute-start(f16[24,1024]{1,0:T(8,128)(2,1)S(1)} %fusion), channel_id=1, source_target_pairs={{0,2},{1,3},{2,0},{3,1},{4,6},{5,7},{6,4},{7,5},{8,10},{9,11},{10,... | collective-permute-start | bytes 147464 | tf_op jit(solution)/shard_map/ppermute | solution.py:225
  36.6 1.3 %collective-permute-start.4 = (bf16[24,1024]{1,0:T(8,128)(2,1)S(1)}, bf16[24,1024]{1,0:T(8,128)(2,1)S(1)}, u32[]{:S(2)}, u32[]{:S(2)}) collective-permute-start(bf16[24,1024]{1,0:T(8,128)(2,1)S(1)} %shard_map.58.own_ref), channel_id=1, source_target_pairs={{0,1},{1,0},{2,3},{3,2},{4,5},{5,4},{6,7},{7,6},{8,9},{9,8},{10,11... | collective-permute-start | bytes 147464 | tf_op jit(solution)/shard_map/ppermute | solution.py:225

commit v6 on v5

--- a/solution.py
+++ b/solution.py
@@ -242,7 +242,7 @@
     slots = grad_slots(held, own, other).astype(jnp.float16)
     slots = lax.all_to_all(slots, "subj", 0, 0)
     factor = -1.0 / (SCALE * float(COUNT * ROWS) ** 0.5)
-    return (jnp.sum(slots.astype(jnp.float32), axis=0) * factor).T
+    return jnp.sum(slots.astype(jnp.float32) * factor, axis=0).T
 
 
 def solution(mesh):

time: 59.8 us -> 59.8 us (level)
    reduce_sum x1, other arithmetic: 0.07 us -> 0.7 us  [per_device(): return jnp.sum(slots.astype(jnp.float32) * factor, axis=0).T]
    mul x1 -> x0, other arithmetic: 0.61 us -> none  [per_device(): return (jnp.sum(slots.astype(jnp.float32), axis=0) * factor).T]
where the time goes in v6:
time: 59.8 us; the launch traced here: 59.7 us
  blocking collectives  41.1 us (69%)
  Pallas kernels  6.82 us (11%)
  waiting for transfers between devices  6.47 us (11%)
  starting transfers between devices  4.44 us (7%)
  other arithmetic  0.79 us (1%)
    all_to_all x1, blocking collectives, per_device(): pack = lax.all_to_all(pack, 'subj', 0, 0)  21.6 us
    all_to_all x1, blocking collectives, per_device(): slots = lax.all_to_all(slots, 'subj', 0, 0)  19.5 us
    ppermute x5, waiting for transfers between devices, swap(): return lax.ppermute(value, 'var', pairs)  6.47 us
    ppermute x5, starting transfers between devices, swap(): return lax.ppermute(value, 'var', pairs)  4.44 us
    pallas_call x1, Pallas kernels, eta_halves(): pl.pallas_call(eta_kernel, in_specs=[hbm(), hbm()], out_specs=[vmem(), vm...  4.27 us
    pallas_call x1, Pallas kernels, grad_slots(): pl.pallas_call(grad_kernel, in_specs=[vmem()] * 3, out_specs=vmem(), out_...  1.55 us
  transfers between devices with their start and end apart: 5, of which 4 were waited for; matrix products, arithmetic and copies ran while one was open for 0% of the time, Pallas kernels for 0%

profile of v6, /device:TPU:32, one launch (start us, length us, event | category | flops | bytes accessed | tf_op | source)
XLA Modules:
  0.0 59.7 jit_solution(5376734616100448727)
XLA Ops:
  0.0 0.0 copy-start
  0.0 0.0 copy-start.1
  0.0 0.0 copy-start.2
  0.0 4.3 %shard_map.55 = (f32[2,24,1024]{2,1,0:T(8,128)S(1)}, bf16[1024,4096]{1,0:T(8,128)(2,1)S(1)}) custom-call(bf16[1024,4096]{1,0:T(8,128)(2,1)} %geno_ref.1, bf16[48,4096]{1,0:T(8,128)(2,1)} %bitcast.16), custom_call_target="tpu_custom_call" | custom-call | flops 1073741824 | bytes 8388608 | tf_op jit(solution)/shard_map/pallas_call | solution.py:67
  4.3 0.1 collective-permute-start
  4.4 1.3 %collective-permute-done = f32[24,1024]{1,0:T(8,128)S(1)} collective-permute-done((f32[24,1024]{1,0:T(8,128)S(1)}, f32[24,1024]{1,0:T(8,128)S(1)}, u32[]{:S(2)}, u32[]{:S(2)}) %collective-permute-start) | collective-permute-done | bytes 98336 | tf_op jit(solution)/shard_map/ppermute | solution.py:225
  5.7 3.1 %collective-permute-start.3 = (f16[24,1024]{1,0:T(8,128)(2,1)S(1)}, f16[24,1024]{1,0:T(8,128)(2,1)S(1)}, u32[]{:S(2)}, u32[]{:S(2)}) collective-permute-start(f16[24,1024]{1,0:T(8,128)(2,1)S(1)} %fusion), channel_id=1, source_target_pairs={{0,4},{1,5},{2,6},{3,7},{4,0},{5,1},{6,2},{7,3},{8,12},{9,13},{10,... | collective-permute-start | bytes 147464 | tf_op jit(solution)/shard_map/ppermute | solution.py:225
  8.8 1.1 %collective-permute-start.2 = (f16[24,1024]{1,0:T(8,128)(2,1)S(1)}, f16[24,1024]{1,0:T(8,128)(2,1)S(1)}, u32[]{:S(2)}, u32[]{:S(2)}) collective-permute-start(f16[24,1024]{1,0:T(8,128)(2,1)S(1)} %fusion), channel_id=1, source_target_pairs={{0,6},{1,7},{2,4},{3,5},{4,2},{5,3},{6,0},{7,1},{8,14},{9,15},{10,... | collective-permute-start | bytes 147464 | tf_op jit(solution)/shard_map/ppermute | solution.py:225
  10.0 0.0 collective-permute-start.1
  10.0 0.0 copy-done
  10.0 0.0 copy-done.1
  10.0 0.0 copy-done.2
  10.0 0.2 shard_map.56
  10.2 1.2 %collective-permute-done.3 = f16[24,1024]{1,0:T(8,128)(2,1)S(1)} collective-permute-done((f16[24,1024]{1,0:T(8,128)(2,1)S(1)}, f16[24,1024]{1,0:T(8,128)(2,1)S(1)}, u32[]{:S(2)}, u32[]{:S(2)}) %collective-permute-start.3) | collective-permute-done | bytes 49184 | tf_op jit(solution)/shard_map/ppermute | solution.py:225
  11.4 2.7 %collective-permute-done.2 = f16[24,1024]{1,0:T(8,128)(2,1)S(1)} collective-permute-done((f16[24,1024]{1,0:T(8,128)(2,1)S(1)}, f16[24,1024]{1,0:T(8,128)(2,1)S(1)}, u32[]{:S(2)}, u32[]{:S(2)}) %collective-permute-start.2) | collective-permute-done | bytes 49184 | tf_op jit(solution)/shard_map/ppermute | solution.py:225
  14.1 0.0 collective-permute-done.1
  14.2 0.2 shard_map.57
  14.4 21.6 %all_to_all.10.pack_ref = bf16[32,24,128]{2,1,0:T(8,128)(2,1)S(1)} all-to-all(bf16[32,24,128]{2,1,0:T(8,128)(2,1)S(1)} %get-tuple-element.20), channel_id=1, replica_groups=mesh['subj'=32,'var'=8] {'subj'}, dimensions={0} | all-to-all | bytes 393216 | tf_op jit(solution)/shard_map/all_to_all | solution.py:239
  35.9 0.6 %shard_map.58.own_ref = bf16[24,1024]{1,0:T(8,128)(2,1)S(1)} custom-call(bf16[32,24,128]{2,1,0:T(8,128)(2,1)S(1)} %all_to_all.10.pack_ref, f32[24,1024]{1,0:T(8,128)S(1)} %get-tuple-element.21.weight_ref, f32[24,1024]{1,0:T(8,128)S(1)} %get-tuple-element.22.counted_ref, bf16[64,1024]{1,0:T(8,128)(2,1)S(1)} %get-tuple-element.23.upto_ref, ...), custom_call_target="tpu_custom_call" | custom-call | flops 100000000 | bytes 1000000 | tf_op jit(solution)/shard_map/pallas_call | solution.py:184
  36.6 0.1 collective-permute-start.4
  36.7 1.2 %collective-permute-done.4.other_ref = bf16[24,1024]{1,0:T(8,128)(2,1)S(1)} collective-permute-done((bf16[24,1024]{1,0:T(8,128)(2,1)S(1)}, bf16[24,1024]{1,0:T(8,128)(2,1)S(1)}, u32[]{:S(2)}, u32[]{:S(2)}) %collective-permute-start.4) | collective-permute-done | bytes 49184 | tf_op jit(solution)/shard_map/ppermute | solution.py:225
  37.9 1.5 %shard_map.59 = f32[32,48,128]{2,1,0:T(8,128)S(1)} custom-call(bf16[1024,4096]{1,0:T(8,128)(2,1)S(1)} %get-tuple-element.15.geno_ref, bf16[24,1024]{1,0:T(8,128)(2,1)S(1)} %shard_map.58.own_ref, bf16[24,1024]{1,0:T(8,128)(2,1)S(1)} %collective-permute-done.4.other_ref), custom_call_target="tpu_custom_call" | custom-call | flops 1073741824 | bytes 8388608 | tf_op jit(solution)/shard_map/pallas_call | solution.py:211
  39.4 0.1 convert_element_type.22
  39.5 19.5 %all_to_all.11 = f16[32,48,128]{2,1,0:T(8,128)(2,1)S(1)} all-to-all(f16[32,48,128]{2,1,0:T(8,128)(2,1)S(1)} %convert_element_type.22), channel_id=1, replica_groups=mesh['subj'=32,'var'=8] {'subj'}, dimensions={0} | all-to-all | bytes 786432 | tf_op jit(solution)/shard_map/all_to_all | solution.py:243
  59.0 0.7 %multiply_reduce_fusion = f32[48,128]{1,0:T(8,128)} fusion(f16[32,48,128]{2,1,0:T(8,128)(2,1)S(1)} %all_to_all.11), kind=kLoop, calls=%fused_computation | loop fusion | flops 583680 | bytes 417792 | tf_op jit(solution)/shard_map/reduce_sum | solution.py:245
  (3 shorter events, 0.1 us)
Async XLA Ops:
  0.0 10.0 %copy-start = (s32[1024,48]{0,1:T(8,128)S(1)}, s32[1024,48]{0,1:T(8,128)}, u32[]{:S(2)}) copy-start(s32[1024,48]{0,1:T(8,128)} %param.8) | copy-start | bytes 589828
  0.0 10.0 %copy-start.1 = (s32[1024]{0:T(1024)S(1)}, s32[1024]{0:T(1024)}, u32[]{:S(2)}) copy-start(s32[1024]{0:T(1024)} %param.7) | copy-start | bytes 12292
  0.0 10.0 %copy-start.2 = (s32[1024]{0:T(1024)S(1)}, s32[1024]{0:T(1024)}, u32[]{:S(2)}) copy-start(s32[1024]{0:T(1024)} %param.9) | copy-start | bytes 12292
  4.3 1.4 %collective-permute-start = (f32[24,1024]{1,0:T(8,128)S(1)}, f32[24,1024]{1,0:T(8,128)S(1)}, u32[]{:S(2)}, u32[]{:S(2)}) collective-permute-start(f32[24,1024]{1,0:T(8,128)S(1)} %slice_bitcast_fusion), channel_id=1, source_target_pairs={{0,1},{1,0},{2,3},{3,2},{4,5},{5,4},{6,7},{7,6},{8,9},{9,8},{10,11... | collective-permute-start | bytes 294920 | tf_op jit(solution)/shard_map/ppermute | solution.py:225
  5.7 5.7 %collective-permute-start.3 = (f16[24,1024]{1,0:T(8,128)(2,1)S(1)}, f16[24,1024]{1,0:T(8,128)(2,1)S(1)}, u32[]{:S(2)}, u32[]{:S(2)}) collective-permute-start(f16[24,1024]{1,0:T(8,128)(2,1)S(1)} %fusion), channel_id=1, source_target_pairs={{0,4},{1,5},{2,6},{3,7},{4,0},{5,1},{6,2},{7,3},{8,12},{9,13},{10,... | collective-permute-start | bytes 147464 | tf_op jit(solution)/shard_map/ppermute | solution.py:225
  8.8 5.3 %collective-permute-start.2 = (f16[24,1024]{1,0:T(8,128)(2,1)S(1)}, f16[24,1024]{1,0:T(8,128)(2,1)S(1)}, u32[]{:S(2)}, u32[]{:S(2)}) collective-permute-start(f16[24,1024]{1,0:T(8,128)(2,1)S(1)} %fusion), channel_id=1, source_target_pairs={{0,6},{1,7},{2,4},{3,5},{4,2},{5,3},{6,0},{7,1},{8,14},{9,15},{10,... | collective-permute-start | bytes 147464 | tf_op jit(solution)/shard_map/ppermute | solution.py:225
  10.0 4.2 %collective-permute-start.1 = (f16[24,1024]{1,0:T(8,128)(2,1)S(1)}, f16[24,1024]{1,0:T(8,128)(2,1)S(1)}, u32[]{:S(2)}, u32[]{:S(2)}) collective-permute-start(f16[24,1024]{1,0:T(8,128)(2,1)S(1)} %fusion), channel_id=1, source_target_pairs={{0,2},{1,3},{2,0},{3,1},{4,6},{5,7},{6,4},{7,5},{8,10},{9,11},{10,... | collective-permute-start | bytes 147464 | tf_op jit(solution)/shard_map/ppermute | solution.py:225
  36.6 1.3 %collective-permute-start.4 = (bf16[24,1024]{1,0:T(8,128)(2,1)S(1)}, bf16[24,1024]{1,0:T(8,128)(2,1)S(1)}, u32[]{:S(2)}, u32[]{:S(2)}) collective-permute-start(bf16[24,1024]{1,0:T(8,128)(2,1)S(1)} %shard_map.58.own_ref), channel_id=1, source_target_pairs={{0,1},{1,0},{2,3},{3,2},{4,5},{5,4},{6,7},{7,6},{8,9},{9,8},{10,11... | collective-permute-start | bytes 147464 | tf_op jit(solution)/shard_map/ppermute | solution.py:225
